TPU v7x, 32 devices: a whole 2x2x4 slice. The times are simulated.
32 devices in a mesh: section: 2 (over core), ctx: 16 (over z, y, x).
Axes of the slice: x: 2, y: 2, z: 4, core: 2. Of those that a mesh axis runs over, the one named last changes fastest.
Arguments:
- queries: bfloat16 [2, 4096, 1024], P('section', 'ctx'), may hold values from -6 to 6
- keys: bfloat16 [2, 4096, 128], P('section', 'ctx'), may hold values from -6 to 6
- values: bfloat16 [2, 4096, 128], P('section', 'ctx'), may hold values from -6 to 6
- attn_out: bfloat16 [2, 4096, 1024], P('section', 'ctx'), may hold values from -3 to 3
- log_sums: float32 [2, 8, 4096], P('section', None, 'ctx'), may hold values from 2 to 6
- grad_held: bfloat16 [2, 4096, 1024], P('section', 'ctx'), may hold values from -6 to 6
- doc_ids: int32 [4096], P('ctx'), may hold values from 0 to 15, never falling along the last dimension, each value on 1 to 512 neighbouring positions
Outputs:
- grad_queries: bfloat16 [2, 4096, 1024], P('section', 'ctx')
- grad_keys: bfloat16 [2, 4096, 128], P('section', 'ctx')
- grad_values: bfloat16 [2, 4096, 128], P('section', 'ctx')
Inputs may be any that keep to these rules, and one draw needn't show every extreme that they name: `doc_ids`: document numbers never fall along the sequence; every document spans at most 512 positions and one spans exactly 512.
All inputs are finite; a program needn't handle non-finite values.
Results may differ from a plain program's by a relative error of at most 0.0049.
Values may be sent and summed in bfloat16 or wider, within the bound.
No kernel may reach another device: no remote copies, remote signals or barrier semaphores. Data moves between devices by JAX's collectives and lax.ppermute only.
A program may use at most 64 MiB of HBM per device.

v0:
```python
import jax
import jax.numpy as jnp
from jax import lax
from jax.sharding import PartitionSpec as P

HOPS = 2


def from_behind(block, axis, distance):
    devices = range(lax.axis_size(axis))
    route = [((i - distance) % len(devices), i) for i in devices]
    return lax.ppermute(block, axis, route)


def shifted(array, axis, by):
    devices = lax.axis_size(axis)
    pairs = [(i, i + by) for i in range(devices) if 0 <= i + by < devices]
    return lax.ppermute(array, axis, pairs)


def pair_scores(query_side, key_side, position_limit, score_scale):
    q_heads, grad_heads, lse_rows, deltas, query_docs, query_pos = query_side
    key_rows, value_rows, key_docs, key_pos = key_side
    scores = (
        jnp.einsum("qhd,kd->hqk", q_heads, key_rows, preferred_element_type=jnp.float32)
        * score_scale
    )
    allowed = (
        (query_docs[:, None] == key_docs[None, :])
        & (key_pos[None, :] <= query_pos[:, None])
        & (key_pos[None, :] >= 0)
        & (query_pos[:, None] < position_limit)
    )
    weights = jnp.where(allowed[None], jnp.exp(scores - lse_rows[:, :, None]), jnp.float32(0.0))
    weight_grads = jnp.einsum(
        "qhd,kd->hqk", grad_heads, value_rows, preferred_element_type=jnp.float32
    )
    score_grads = (weights * (weight_grads - deltas[:, :, None])).astype(jnp.bfloat16)
    return (weights.astype(jnp.bfloat16), score_grads)


def query_part(score_grads, key_rows, score_scale):
    return (
        jnp.einsum("hqk,kd->qhd", score_grads, key_rows, preferred_element_type=jnp.float32)
        * score_scale
    )


def key_part(weights_low, score_grads, q_heads, grad_heads, score_scale):
    grad_k = (
        jnp.einsum("hqk,qhd->kd", score_grads, q_heads, preferred_element_type=jnp.float32)
        * score_scale
    )
    grad_v = jnp.einsum("hqk,qhd->kd", weights_low, grad_heads, preferred_element_type=jnp.float32)
    return (grad_k, grad_v)


def per_device(queries, keys, values, attn_out, log_sums, grad_held, doc_ids):
    arrived = from_behind(grad_held, "section", -1)
    row_count = queries.shape[1]
    head_count = log_sums.shape[1]
    head_width = keys.shape[2]
    score_scale = float(head_width) ** (-0.5)
    q_heads = queries[0].reshape(row_count, head_count, head_width)
    grad_heads = arrived[0].reshape(row_count, head_count, head_width)
    out_heads = attn_out[0].reshape(row_count, head_count, head_width)
    lse_rows = log_sums[0]
    deltas = jnp.einsum("qhd,qhd->hq", grad_heads, out_heads, preferred_element_type=jnp.float32)
    key_rows = keys[0]
    value_rows = values[0]
    shard_index = lax.axis_index("ctx")
    position_limit = lax.axis_size("ctx") * row_count
    offsets = jnp.arange(row_count, dtype=jnp.int32)
    query_pos = shard_index * row_count + offsets
    query_side = (q_heads, grad_heads, lse_rows, deltas, doc_ids, query_pos)
    own_side = (key_rows, value_rows, doc_ids, query_pos)
    weights_low, score_grads = pair_scores(query_side, own_side, position_limit, score_scale)
    grad_q = query_part(score_grads, key_rows, score_scale)
    grad_k, grad_v = key_part(weights_low, score_grads, q_heads, grad_heads, score_scale)
    remote = []
    for distance in range(1, HOPS + 1):
        remote.append(shifted((key_rows, value_rows, doc_ids), "ctx", distance))
    key_terms = []
    for distance in range(1, HOPS + 1):
        far_keys, far_values, far_docs = remote[distance - 1]
        key_pos = (shard_index - distance) * row_count + offsets
        far_side = (far_keys, far_values, far_docs, key_pos)
        far_weights, far_grads = pair_scores(query_side, far_side, position_limit, score_scale)
        grad_q = grad_q + query_part(far_grads, far_keys, score_scale)
        key_terms.append(key_part(far_weights, far_grads, q_heads, grad_heads, score_scale))
    for distance in range(1, HOPS + 1):
        back_keys, back_values = shifted(key_terms[distance - 1], "ctx", -distance)
        grad_k = grad_k + back_keys
        grad_v = grad_v + back_values
    grad_queries = grad_q.reshape(row_count, head_count * head_width).astype(jnp.bfloat16)[None]
    return (grad_queries, grad_k.astype(jnp.bfloat16)[None], grad_v.astype(jnp.bfloat16)[None])


def solution(mesh):
    placed = (
        P("section", "ctx", None),
        P("section", "ctx", None),
        P("section", "ctx", None),
        P("section", "ctx", None),
        P("section", None, "ctx"),
        P("section", "ctx", None),
        P("ctx"),
    )
    return jax.shard_map(
        per_device,
        mesh=mesh,
        in_specs=placed,
        out_specs=(P("section", "ctx", None), P("section", "ctx", None), P("section", "ctx", None)),
        check_vma=False,
    )
```

profile of v0, /device:TPU:0, one launch (start us, length us, event | category | flops | bytes accessed | tf_op | source)
XLA Modules:
  0.0 61.9 jit_solution(9835531991339943436)
XLA Ops:
  0.6 0.0 copy-start.7
  0.7 5.0 %collective-permute-start.4 = (s32[256]{0:T(256)}, s32[256]{0:T(256)S(1)}, u32[]{:S(2)}, u32[]{:S(2)}) collective-permute-start(s32[256]{0:T(256)} %param.13), channel_id=1, source_target_pairs={{0,2},{1,3},{2,4},{3,5},{4,6},{5,7},{6,8},{7,9},{8,10},{9,11},{10,... | collective-permute-start | bytes 3080 | tf_op jit(solution)/shard_map/ppermute | solution.py:18
  5.7 3.4 %collective-permute-start.1 = (s32[256]{0:T(256)}, s32[256]{0:T(256)S(1)}, u32[]{:S(2)}, u32[]{:S(2)}) collective-permute-start(s32[256]{0:T(256)} %param.13), channel_id=1, source_target_pairs={{0,1},{1,2},{2,3},{3,4},{4,5},{5,6},{6,7},{7,8},{8,9},{9,10},{10,1... | collective-permute-start | bytes 3080 | tf_op jit(solution)/shard_map/ppermute | solution.py:18
  9.1 3.4 %collective-permute-start.3 = (bf16[256,128]{1,0:T(8,128)(2,1)}, bf16[256,128]{1,0:T(8,128)(2,1)S(1)}, u32[]{:S(2)}, u32[]{:S(2)}) collective-permute-start(bf16[256,128]{1,0:T(8,128)(2,1)} %bitcast.148), channel_id=1, source_target_pairs={{0,1},{1,2},{2,3},{3,4},{4,5},{5,6},{6,7},{7,8},{8,9},{9,10},{10,1... | collective-permute-start | bytes 196616 | tf_op jit(solution)/shard_map/ppermute | solution.py:18
  12.5 4.0 %collective-permute-start.6 = (bf16[256,128]{1,0:T(8,128)(2,1)}, bf16[256,128]{1,0:T(8,128)(2,1)}, u32[]{:S(2)}, u32[]{:S(2)}) collective-permute-start(bf16[256,128]{1,0:T(8,128)(2,1)} %bitcast.149), channel_id=1, source_target_pairs={{0,2},{1,3},{2,4},{3,5},{4,6},{5,7},{6,8},{7,9},{8,10},{9,11},{10,... | collective-permute-start | bytes 196616 | tf_op jit(solution)/shard_map/ppermute | solution.py:18
  16.6 3.4 %collective-permute-start.2 = (bf16[256,128]{1,0:T(8,128)(2,1)}, bf16[256,128]{1,0:T(8,128)(2,1)S(1)}, u32[]{:S(2)}, u32[]{:S(2)}) collective-permute-start(bf16[256,128]{1,0:T(8,128)(2,1)} %bitcast.150), channel_id=1, source_target_pairs={{0,1},{1,2},{2,3},{3,4},{4,5},{5,6},{6,7},{7,8},{8,9},{9,10},{10,1... | collective-permute-start | bytes 196616 | tf_op jit(solution)/shard_map/ppermute | solution.py:18
  20.0 1.1 %copy.65 = bf16[32,8,8,128]{3,2,1,0:T(8,128)(2,1)S(1)} copy(bf16[32,8,8,128]{3,1,2,0:T(8,128)(2,1)} %bitcast.146) | data formatting | bytes 1048576
  21.2 1.3 %copy.66 = bf16[32,8,8,128]{3,2,1,0:T(8,128)(2,1)S(1)} copy(bf16[32,8,8,128]{3,1,2,0:T(8,128)(2,1)} %bitcast.147) | data formatting | bytes 1048576
  22.5 1.0 %copy.24 = bf16[1,256,1024]{1,2,0:T(8,128)(2,1)} copy(bf16[1,256,1024]{2,1,0:T(8,128)(2,1)S(1)} %copy-done.5) | data formatting | bytes 1048576 | tf_op args[5]
  23.5 0.0 collective-permute-done.4
  23.5 2.8 %collective-permute-start.5 = (bf16[256,128]{1,0:T(8,128)(2,1)S(1)}, bf16[256,128]{1,0:T(8,128)(2,1)S(1)}, u32[]{:S(2)}, u32[]{:S(2)}) collective-permute-start(bf16[256,128]{1,0:T(8,128)(2,1)S(1)} %bitcast.151), channel_id=1, source_target_pairs={{0,2},{1,3},{2,4},{3,5},{4,6},{5,7},{6,8},{7,9},{8,10},{9,11},{10,... | collective-permute-start | bytes 196616 | tf_op jit(solution)/shard_map/ppermute | solution.py:18
  26.3 0.0 collective-permute-done.1
  26.3 0.1 collective-permute-start
  26.4 0.6 and_and_fusion
  27.0 1.9 %fusion.11 = f32[8,256,256]{1,2,0:T(8,128)} fusion(f32[8,256]{1,0:T(8,128)S(1)} %bitcast.152, pred[256,256]{0,1:T(8,128)(4,1)S(1)} %get-tuple-element.10, bf16[256,8,128]{2,1,0:T(8,128)(2,1)S(1)} %bitcast.139, bf16[1,256,128]{2,1,0:T(8,128)(2,1)S(1)} %copy-done.7), kind=kOutput, calls=%fused_computation.17 | convolution fusion | flops 135790592 | bytes 2760704 | tf_op jit(solution)/shard_map/qhd,kd->hqk/dot_general | solution.py:25
  29.0 0.0 collective-permute-done.2
  29.0 1.9 %fusion.7 = f32[8,256,256]{1,2,0:T(8,128)} fusion(f32[8,256]{1,0:T(8,128)S(1)} %bitcast.153, pred[256,256]{0,1:T(8,128)(4,1)S(1)} %get-tuple-element.11, bf16[256,8,128]{2,1,0:T(8,128)(2,1)S(1)} %bitcast.140, bf16[256,128]{1,0:T(8,128)(2,1)S(1)} %collective-permute-done.2), kind=kOutput, calls=%fused_computation.11 | convolution fusion | flops 135790592 | bytes 2760704 | tf_op jit(solution)/shard_map/qhd,kd->hqk/dot_general | solution.py:25
  30.9 0.0 collective-permute-done.5
  30.9 1.7 %fusion.3 = f32[8,256,256]{1,2,0:T(8,128)S(1)} fusion(f32[8,256]{1,0:T(8,128)S(1)} %bitcast.154, pred[256,256]{0,1:T(8,128)(4,1)S(1)} %get-tuple-element.9, bf16[256,8,128]{2,1,0:T(8,128)(2,1)} %bitcast.141, bf16[256,128]{1,0:T(8,128)(2,1)S(1)} %collective-permute-done.5), kind=kOutput, calls=%fused_computation.5 | convolution fusion | flops 135790592 | bytes 2760704 | tf_op jit(solution)/shard_map/qhd,kd->hqk/dot_general | solution.py:25
  32.6 0.0 collective-permute-done
  32.6 1.2 %copy.49 = f32[8,256,128]{2,0,1:T(8,128)} copy(bf16[8,256,128]{1,2,0:T(8,128)(2,1)S(1)} %bitcast.131) | data formatting | bytes 1572864
  33.8 2.1 %convolution_bitcast_fusion.1 = f32[256,128]{1,0:T(8,128)S(1)} fusion(bf16[256,8,128]{0,2,1:T(8,128)(2,1)S(1)} %bitcast.132, f32[8,256,256]{1,2,0:T(8,128)} %fusion.7), kind=kOutput, calls=%fused_computation.23 | convolution fusion | flops 134742016 | bytes 2752512 | tf_op jit(solution)/shard_map/hqk,qhd->kd/dot_general | solution.py:54
  36.0 0.3 multiply_reduce_fusion
  36.3 0.1 copy.50
  36.4 0.0 collective-permute-done.3
  36.4 2.1 %fusion.5 = bf16[8,256,256]{1,2,0:T(8,128)(2,1)S(1)} fusion(f32[8,256,256]{1,2,0:T(8,128)} %fusion.7, bf16[256,8,128]{0,2,1:T(8,128)(2,1)S(1)} %bitcast.133, f32[8,256]{1,0:T(8,128)S(1)} %copy.50, bf16[256,128]{1,0:T(8,128)(2,1)S(1)} %collective-permute-done.3), kind=kOutput, calls=%fused_computation.8 | convolution fusion | flops 135790592 | bytes 3743744 | tf_op jit(solution)/shard_map/qhd,kd->hqk/dot_general | solution.py:35
  38.5 1.1 %fusion.15 = f32[256,128]{1,0:T(8,128)} fusion(bf16[8,256,256]{1,2,0:T(8,128)(2,1)S(1)} %fusion.5, bf16[256,8,128]{2,1,0:T(8,128)(2,1)S(1)} %bitcast.142), kind=kOutput, calls=%fused_computation.28 | convolution fusion | flops 134250496 | bytes 1703936 | tf_op jit(solution)/shard_map/hqk,qhd->kd/dot_general | solution.py:51
  39.5 1.3 %collective-permute-start.7 = (f32[256,128]{1,0:T(8,128)}, f32[256,128]{1,0:T(8,128)S(1)}, u32[]{:S(2)}, u32[]{:S(2)}) collective-permute-start(f32[256,128]{1,0:T(8,128)} %fusion.15), channel_id=1, source_target_pairs={{1,0},{2,1},{3,2},{4,3},{5,4},{6,5},{7,6},{8,7},{9,8},{10,9},{11,1... | collective-permute-start | bytes 393224 | tf_op jit(solution)/shard_map/ppermute | solution.py:18
  40.8 1.3 %collective-permute-start.9 = (f32[256,128]{1,0:T(8,128)S(1)}, f32[256,128]{1,0:T(8,128)S(1)}, u32[]{:S(2)}, u32[]{:S(2)}) collective-permute-start(f32[256,128]{1,0:T(8,128)S(1)} %convolution_bitcast_fusion.1), channel_id=1, source_target_pairs={{1,0},{2,1},{3,2},{4,3},{5,4},{6,5},{7,6},{8,7},{9,8},{10,9},{11,1... | collective-permute-start | bytes 393224 | tf_op jit(solution)/shard_map/ppermute | solution.py:18
  42.1 1.1 %convolution_bitcast_fusion = f32[256,128]{1,0:T(8,128)} fusion(bf16[256,8,128]{0,2,1:T(8,128)(2,1)S(1)} %bitcast.134, f32[8,256,256]{1,2,0:T(8,128)S(1)} %fusion.3), kind=kOutput, calls=%fused_computation.22 | convolution fusion | flops 134742016 | bytes 2752512 | tf_op jit(solution)/shard_map/hqk,qhd->kd/dot_general | solution.py:54
  43.2 0.0 collective-permute-done.6
  43.2 1.4 %fusion.1 = bf16[8,256,256]{1,2,0:T(8,128)(2,1)S(1)} fusion(f32[8,256,256]{1,2,0:T(8,128)S(1)} %fusion.3, bf16[256,8,128]{0,2,1:T(8,128)(2,1)S(1)} %bitcast.135, f32[8,256]{1,0:T(8,128)S(1)} %copy.50, bf16[256,128]{1,0:T(8,128)(2,1)} %collective-permute-done.6), kind=kOutput, calls=%fused_computation.2 | convolution fusion | flops 135790592 | bytes 3743744 | tf_op jit(solution)/shard_map/qhd,kd->hqk/dot_general | solution.py:35
  44.6 0.4 fusion.14
  45.1 0.0 copy-start.8
  45.1 0.0 copy-start.10
  45.1 1.4 %collective-permute-start.8 = (f32[256,128]{1,0:T(8,128)S(1)}, f32[256,128]{1,0:T(8,128)S(1)}, u32[]{:S(2)}, u32[]{:S(2)}) collective-permute-start(f32[256,128]{1,0:T(8,128)S(1)} %fusion.14), channel_id=1, source_target_pairs={{2,0},{3,1},{4,2},{5,3},{6,4},{7,5},{8,6},{9,7},{10,8},{11,9},{12,... | collective-permute-start | bytes 393224 | tf_op jit(solution)/shard_map/ppermute | solution.py:18
  46.5 1.3 %collective-permute-start.10 = (f32[256,128]{1,0:T(8,128)}, f32[256,128]{1,0:T(8,128)S(1)}, u32[]{:S(2)}, u32[]{:S(2)}) collective-permute-start(f32[256,128]{1,0:T(8,128)} %convolution_bitcast_fusion), channel_id=1, source_target_pairs={{2,0},{3,1},{4,2},{5,3},{6,4},{7,5},{8,6},{9,7},{10,8},{11,9},{12,... | collective-permute-start | bytes 393224 | tf_op jit(solution)/shard_map/ppermute | solution.py:18
  47.8 0.4 fusion.9
  48.3 0.3 fusion.41
  48.6 0.0 copy-start.12
  48.6 0.4 convolution_add_fusion.1
  49.0 0.5 copy-done.12
  49.5 0.4 fusion.13
  49.9 1.0 %copy.42 = bf16[1,256,1024]{2,1,0:T(8,128)(2,1)} copy(bf16[1,256,1024]{1,2,0:T(8,128)(2,1)S(1)} %bitcast.145) | data formatting | bytes 1048576
  50.9 7.3 %collective-permute-done.10 = f32[256,128]{1,0:T(8,128)S(1)} collective-permute-done((f32[256,128]{1,0:T(8,128)}, f32[256,128]{1,0:T(8,128)S(1)}, u32[]{:S(2)}, u32[]{:S(2)}) %collective-permute-start.10) | collective-permute-done | bytes 131104 | tf_op jit(solution)/shard_map/ppermute | solution.py:18
  58.2 2.7 %fusion.24 = bf16[1,256,128]{2,1,0:T(8,128)(2,1)} fusion(f32[256,128]{1,0:T(8,128)S(1)} %collective-permute-done.10, f32[256,128]{1,0:T(8,128)S(1)} %collective-permute-done.9, bf16[256,8,128]{0,2,1:T(8,128)(2,1)S(1)} %bitcast.137, f32[8,256,256]{1,2,0:T(8,128)} %fusion.11), kind=kOutput, calls=%fused_computation.38 | convolution fusion | flops 134840320 | bytes 2949120 | tf_op jit(solution)/shard_map/hqk,qhd->kd/dot_general | solution.py:54
  60.8 0.0 collective-permute-done.8
  60.9 1.1 %fusion.23 = bf16[1,256,128]{2,1,0:T(8,128)(2,1)} fusion(f32[256,128]{1,0:T(8,128)S(1)} %collective-permute-done.8, f32[256,128]{1,0:T(8,128)S(1)} %collective-permute-done.7, bf16[8,256,256]{1,2,0:T(8,128)(2,1)S(1)} %fusion.9, bf16[256,8,128]{2,1,0:T(8,128)(2,1)S(1)} %bitcast.144), kind=kOutput, calls=%fused_computation.37 | convolution fusion | flops 134348800 | bytes 1900544 | tf_op jit(solution)/shard_map/hqk,qhd->kd/dot_general | solution.py:51
  (31 shorter events, 0.1 us)
Async XLA Ops:
  0.6 25.8 %copy-start.13 = (s32[256]{0:T(256)S(1)}, s32[256]{0:T(256)}, u32[]{:S(2)}) copy-start(s32[256]{0:T(256)} %param.13) | copy-start | bytes 3076
  0.6 22.9 %copy-start.7 = (bf16[1,256,128]{2,1,0:T(8,128)(2,1)S(1)}, bf16[1,256,128]{2,1,0:T(8,128)(2,1)}, u32[]{:S(2)}) copy-start(bf16[1,256,128]{2,1,0:T(8,128)(2,1)} %param.8) | copy-start | bytes 196612
  0.7 21.8 %copy-start.5 = (bf16[1,256,1024]{2,1,0:T(8,128)(2,1)S(1)}, bf16[1,256,1024]{2,1,0:T(8,128)(2,1)}, u32[]{:S(2)}) copy-start(bf16[1,256,1024]{2,1,0:T(8,128)(2,1)} %param.12) | copy-start | bytes 1572868
  0.7 26.3 %copy-start.14 = (f32[1,8,256]{2,1,0:T(8,128)S(1)}, f32[1,8,256]{2,1,0:T(8,128)}, u32[]{:S(2)}) copy-start(f32[1,8,256]{2,1,0:T(8,128)} %param.11) | copy-start | bytes 24580
  0.7 22.8 %collective-permute-start.4 = (s32[256]{0:T(256)}, s32[256]{0:T(256)S(1)}, u32[]{:S(2)}, u32[]{:S(2)}) collective-permute-start(s32[256]{0:T(256)} %param.13), channel_id=1, source_target_pairs={{0,2},{1,3},{2,4},{3,5},{4,6},{5,7},{6,8},{7,9},{8,10},{9,11},{10,... | collective-permute-start | bytes 3080 | tf_op jit(solution)/shard_map/ppermute | solution.py:18
  5.7 20.7 %collective-permute-start.1 = (s32[256]{0:T(256)}, s32[256]{0:T(256)S(1)}, u32[]{:S(2)}, u32[]{:S(2)}) collective-permute-start(s32[256]{0:T(256)} %param.13), channel_id=1, source_target_pairs={{0,1},{1,2},{2,3},{3,4},{4,5},{5,6},{6,7},{7,8},{8,9},{9,10},{10,1... | collective-permute-start | bytes 3080 | tf_op jit(solution)/shard_map/ppermute | solution.py:18
  9.1 27.3 %collective-permute-start.3 = (bf16[256,128]{1,0:T(8,128)(2,1)}, bf16[256,128]{1,0:T(8,128)(2,1)S(1)}, u32[]{:S(2)}, u32[]{:S(2)}) collective-permute-start(bf16[256,128]{1,0:T(8,128)(2,1)} %bitcast.148), channel_id=1, source_target_pairs={{0,1},{1,2},{2,3},{3,4},{4,5},{5,6},{6,7},{7,8},{8,9},{9,10},{10,1... | collective-permute-start | bytes 196616 | tf_op jit(solution)/shard_map/ppermute | solution.py:18
  12.5 30.7 %collective-permute-start.6 = (bf16[256,128]{1,0:T(8,128)(2,1)}, bf16[256,128]{1,0:T(8,128)(2,1)}, u32[]{:S(2)}, u32[]{:S(2)}) collective-permute-start(bf16[256,128]{1,0:T(8,128)(2,1)} %bitcast.149), channel_id=1, source_target_pairs={{0,2},{1,3},{2,4},{3,5},{4,6},{5,7},{6,8},{7,9},{8,10},{9,11},{10,... | collective-permute-start | bytes 196616 | tf_op jit(solution)/shard_map/ppermute | solution.py:18
  16.6 12.4 %collective-permute-start.2 = (bf16[256,128]{1,0:T(8,128)(2,1)}, bf16[256,128]{1,0:T(8,128)(2,1)S(1)}, u32[]{:S(2)}, u32[]{:S(2)}) collective-permute-start(bf16[256,128]{1,0:T(8,128)(2,1)} %bitcast.150), channel_id=1, source_target_pairs={{0,1},{1,2},{2,3},{3,4},{4,5},{5,6},{6,7},{7,8},{8,9},{9,10},{10,1... | collective-permute-start | bytes 196616 | tf_op jit(solution)/shard_map/ppermute | solution.py:18
  21.2 7.8 %copy-start.2 = (bf16[32,8,8,128]{3,2,1,0:T(8,128)(2,1)}, bf16[32,8,8,128]{3,2,1,0:T(8,128)(2,1)S(1)}, u32[]{:S(2)}) copy-start(bf16[32,8,8,128]{3,2,1,0:T(8,128)(2,1)S(1)} %copy.65) | copy-start | bytes 1572868
  23.5 7.4 %collective-permute-start.5 = (bf16[256,128]{1,0:T(8,128)(2,1)S(1)}, bf16[256,128]{1,0:T(8,128)(2,1)S(1)}, u32[]{:S(2)}, u32[]{:S(2)}) collective-permute-start(bf16[256,128]{1,0:T(8,128)(2,1)S(1)} %bitcast.151), channel_id=1, source_target_pairs={{0,2},{1,3},{2,4},{3,5},{4,6},{5,7},{6,8},{7,9},{8,10},{9,11},{10,... | collective-permute-start | bytes 196616 | tf_op jit(solution)/shard_map/ppermute | solution.py:18
  26.3 6.2 %collective-permute-start = (bf16[1,256,1024]{1,2,0:T(8,128)(2,1)}, bf16[1,256,1024]{1,2,0:T(8,128)(2,1)S(1)}, u32[]{:S(2)}, u32[]{:S(2)}) collective-permute-start(bf16[1,256,1024]{1,2,0:T(8,128)(2,1)} %copy.24), channel_id=1, source_target_pairs={{16,0},{0,16},{17,1},{1,17},{18,2},{2,18},{19,3},{3,19},{20,4},{4,... | collective-permute-start | bytes 1572872 | tf_op jit(solution)/shard_map/ppermute | solution.py:12
  29.0 1.9 %copy-start.9 = (bf16[256,128]{1,0:T(8,128)(2,1)}, bf16[256,128]{1,0:T(8,128)(2,1)S(1)}, u32[]{:S(2)}) copy-start(bf16[256,128]{1,0:T(8,128)(2,1)S(1)} %collective-permute-done.2) | copy-start | bytes 196612
  30.9 1.7 %copy-start.11 = (bf16[256,128]{1,0:T(8,128)(2,1)}, bf16[256,128]{1,0:T(8,128)(2,1)S(1)}, u32[]{:S(2)}) copy-start(bf16[256,128]{1,0:T(8,128)(2,1)S(1)} %collective-permute-done.5) | copy-start | bytes 196612
  33.8 2.1 %copy-start.1 = (f32[8,256,128]{2,0,1:T(8,128)S(1)}, f32[8,256,128]{2,0,1:T(8,128)}, u32[]{:S(2)}) copy-start(f32[8,256,128]{2,0,1:T(8,128)} %copy.49) | copy-start | bytes 3145732
  36.3 2.2 %copy-start.3 = (bf16[32,8,8,128]{3,2,1,0:T(8,128)(2,1)S(1)}, bf16[32,8,8,128]{3,2,1,0:T(8,128)(2,1)}, u32[]{:S(2)}) copy-start(bf16[32,8,8,128]{3,2,1,0:T(8,128)(2,1)} %copy-done.2) | copy-start | bytes 1572868
  39.5 21.3 %collective-permute-start.7 = (f32[256,128]{1,0:T(8,128)}, f32[256,128]{1,0:T(8,128)S(1)}, u32[]{:S(2)}, u32[]{:S(2)}) collective-permute-start(f32[256,128]{1,0:T(8,128)} %fusion.15), channel_id=1, source_target_pairs={{1,0},{2,1},{3,2},{4,3},{5,4},{6,5},{7,6},{8,7},{9,8},{10,9},{11,1... | collective-permute-start | bytes 393224 | tf_op jit(solution)/shard_map/ppermute | solution.py:18
  40.8 10.0 %collective-permute-start.9 = (f32[256,128]{1,0:T(8,128)S(1)}, f32[256,128]{1,0:T(8,128)S(1)}, u32[]{:S(2)}, u32[]{:S(2)}) collective-permute-start(f32[256,128]{1,0:T(8,128)S(1)} %convolution_bitcast_fusion.1), channel_id=1, source_target_pairs={{1,0},{2,1},{3,2},{4,3},{5,4},{6,5},{7,6},{8,7},{9,8},{10,9},{11,1... | collective-permute-start | bytes 393224 | tf_op jit(solution)/shard_map/ppermute | solution.py:18
  43.2 4.6 %copy-start = (f32[8,256,256]{1,2,0:T(8,128)S(1)}, f32[8,256,256]{1,2,0:T(8,128)}, u32[]{:S(2)}) copy-start(f32[8,256,256]{1,2,0:T(8,128)} %fusion.11) | copy-start | bytes 6291460
  43.2 4.6 %copy-start.6 = (bf16[1,256,128]{2,1,0:T(8,128)(2,1)S(1)}, bf16[1,256,128]{2,1,0:T(8,128)(2,1)}, u32[]{:S(2)}) copy-start(bf16[1,256,128]{2,1,0:T(8,128)(2,1)} %param.9) | copy-start | bytes 196612
  45.1 3.2 %copy-start.8 = (bf16[1,256,128]{2,1,0:T(8,128)(2,1)S(1)}, bf16[1,256,128]{2,1,0:T(8,128)(2,1)}, u32[]{:S(2)}) copy-start(bf16[1,256,128]{2,1,0:T(8,128)(2,1)} %param.8) | copy-start | bytes 196612
  45.1 3.6 %copy-start.10 = (bf16[256,128]{1,0:T(8,128)(2,1)S(1)}, bf16[256,128]{1,0:T(8,128)(2,1)}, u32[]{:S(2)}) copy-start(bf16[256,128]{1,0:T(8,128)(2,1)} %copy-done.9) | copy-start | bytes 196612
  45.1 15.8 %collective-permute-start.8 = (f32[256,128]{1,0:T(8,128)S(1)}, f32[256,128]{1,0:T(8,128)S(1)}, u32[]{:S(2)}, u32[]{:S(2)}) collective-permute-start(f32[256,128]{1,0:T(8,128)S(1)} %fusion.14), channel_id=1, source_target_pairs={{2,0},{3,1},{4,2},{5,3},{6,4},{7,5},{8,6},{9,7},{10,8},{11,9},{12,... | collective-permute-start | bytes 393224 | tf_op jit(solution)/shard_map/ppermute | solution.py:18
  46.5 11.7 %collective-permute-start.10 = (f32[256,128]{1,0:T(8,128)}, f32[256,128]{1,0:T(8,128)S(1)}, u32[]{:S(2)}, u32[]{:S(2)}) collective-permute-start(f32[256,128]{1,0:T(8,128)} %convolution_bitcast_fusion), channel_id=1, source_target_pairs={{2,0},{3,1},{4,2},{5,3},{6,4},{7,5},{8,6},{9,7},{10,8},{11,9},{12,... | collective-permute-start | bytes 393224 | tf_op jit(solution)/shard_map/ppermute | solution.py:18
  48.6 0.8 %copy-start.12 = (bf16[256,128]{1,0:T(8,128)(2,1)S(1)}, bf16[256,128]{1,0:T(8,128)(2,1)}, u32[]{:S(2)}) copy-start(bf16[256,128]{1,0:T(8,128)(2,1)} %copy-done.11) | copy-start | bytes 196612
  49.8 11.0 %copy-start.4 = (bf16[32,8,8,128]{3,2,1,0:T(8,128)(2,1)S(1)}, bf16[32,8,8,128]{3,2,1,0:T(8,128)(2,1)}, u32[]{:S(2)}) copy-start(bf16[32,8,8,128]{3,2,1,0:T(8,128)(2,1)} %copy-done.2) | copy-start | bytes 1572868
where the time goes:
time: 62.7 us; the launch traced here: 61.9 us
  starting transfers between devices  27.4 us (44%)
  matrix products  18.9 us (30%)
  waiting for transfers between devices  7.34 us (12%)
  local copies, waits for them, and re-layouts  6.29 us (10%)
  between operations  1.03 us (2%)
  other arithmetic  0.93 us (1%)
    ppermute x10, starting transfers between devices, shifted(): return lax.ppermute(array, axis, pairs)  27.4 us
    ppermute x10, waiting for transfers between devices, shifted(): return lax.ppermute(array, axis, pairs)  7.34 us
    unnamed x35, local copies, waits for them, and re-layouts  6.24 us
    dot_general x3, matrix products, key_part(): jnp.einsum('hqk,qhd->kd', weights_low, grad_heads, preferred_element_type...  5.84 us
    dot_general x3, matrix products, pair_scores(): jnp.einsum('qhd,kd->hqk', q_heads, key_rows, preferred_element_type=jnp.f...  5.53 us
    dot_general x3, matrix products, pair_scores(): jnp.einsum('qhd,kd->hqk', grad_heads, value_rows, preferred_element_type=...  3.9 us
    dot_general x3, matrix products, key_part(): jnp.einsum('hqk,qhd->kd', score_grads, q_heads, preferred_element_type=jn...  2.55 us
  transfers between devices with their start and end apart: 11, of which 1 were waited for; matrix products, arithmetic and copies ran while one was open for 40% of the time, Pallas kernels for 0%

commit v1 on v0

v1 whole, which is shorter than its diff:
```python
import functools

import jax
import jax.numpy as jnp
from jax import lax
from jax.experimental import pallas as pl
from jax.experimental.pallas import tpu as pltpu
from jax.sharding import PartitionSpec as P

HOPS = 2
DOC_ROWS = 16
LOG2_E = 1.4426950408889634
MASKED = -1e30

F32 = jnp.float32
BF16 = jnp.bfloat16


def from_behind(block, axis, distance):
    devices = range(lax.axis_size(axis))
    route = [((i - distance) % len(devices), i) for i in devices]
    return lax.ppermute(block, axis, route)


def shifted(array, axis, by):
    devices = lax.axis_size(axis)
    pairs = [(i, i + by) for i in range(devices) if 0 <= i + by < devices]
    return lax.ppermute(array, axis, pairs)


def dot_nt(a, b):
    return lax.dot_general(a, b, (((1,), (1,)), ((), ())), preferred_element_type=F32)


def dot_nn(a, b):
    return lax.dot_general(a, b, (((1,), (0,)), ((), ())), preferred_element_type=F32)


def vmem(count):
    return [pl.BlockSpec(memory_space=pltpu.VMEM)] * count


def pack_kernel(keys, values, docs, packed):
    rows, width = keys.shape[1:]
    packed[0:rows, 0:width] = keys[0]
    packed[0:rows, width : 2 * width] = values[0]
    docs_row = docs[...].astype(F32).astype(BF16)
    packed[rows : rows + DOC_ROWS, :] = jnp.broadcast_to(docs_row, (DOC_ROWS, docs_row.shape[1]))


def grads_kernel(place, queries, attn_out, grads, log_sums, docs, own, near, far, dq, own_sums, near_sums, far_sums, bias):
    rows = queries.shape[1]
    heads = log_sums.shape[1]
    width = queries.shape[2] // heads
    scale = float(width) ** -0.5
    blocks = (own, near, far)
    shard = place[0]

    docs_row = docs[...].astype(F32)
    docs_col = jnp.transpose(jnp.broadcast_to(docs_row, (width, rows)))
    docs_col = jnp.concatenate([docs_col] * (rows // width), axis=1)
    key_at = lax.broadcasted_iota(jnp.int32, (rows, rows), 0)
    query_at = lax.broadcasted_iota(jnp.int32, (rows, rows), 1)
    bias[0] = jnp.where((docs_col == docs_row) & (key_at <= query_at), 0.0, MASKED)
    for hop in range(1, HOPS + 1):
        far_docs = blocks[hop][rows : rows + DOC_ROWS, :].astype(F32)[0:1]
        far_col = jnp.transpose(jnp.broadcast_to(far_docs, (width, rows)))
        far_col = jnp.concatenate([far_col] * (rows // width), axis=1)
        bias[hop] = jnp.where((far_col == docs_row) & (shard >= hop), 0.0, MASKED)

    sums_k = [None] * (HOPS + 1)
    sums_v = [None] * (HOPS + 1)
    keys_turned = [jnp.transpose(block[0:rows, 0:width].astype(F32)).astype(BF16) for block in blocks]
    one = jnp.ones((8, width), BF16)
    for head in range(heads):
        part = slice(head * width, (head + 1) * width)
        q = queries[0, :, part]
        g = grads[0, :, part]
        product = g.astype(F32) * attn_out[0, :, part].astype(F32)
        high = product.astype(BF16)
        low = (product - high.astype(F32)).astype(BF16)
        delta = (dot_nt(one, high) + dot_nt(one, low))[0:1]
        lse = log_sums[0, head : head + 1, :] * LOG2_E
        dq_turned = None
        for hop in range(HOPS + 1):
            block = blocks[hop]
            scores = dot_nt(block[0:rows, 0:width], q)
            weights = jnp.exp2(scores * (scale * LOG2_E) - lse + bias[hop])
            weight_grads = dot_nt(block[0:rows, width : 2 * width], g)
            score_grads = (weights * (weight_grads - delta)).astype(BF16)
            term_v = dot_nn(weights.astype(BF16), g)
            term_k = dot_nn(score_grads, q)
            term_q = dot_nn(keys_turned[hop], score_grads)
            sums_v[hop] = term_v if head == 0 else sums_v[hop] + term_v
            sums_k[hop] = term_k if head == 0 else sums_k[hop] + term_k
            dq_turned = term_q if hop == 0 else dq_turned + term_q
        dq[0, :, part] = jnp.transpose(dq_turned * scale).astype(BF16)
    for hop, out in enumerate((own_sums, near_sums, far_sums)):
        out[:, 0:width] = (sums_k[hop] * scale).astype(out.dtype)
        out[:, width : 2 * width] = sums_v[hop].astype(out.dtype)


def add_kernel(own_sums, near_sums, far_sums, grad_keys, grad_values):
    width = grad_keys.shape[2]
    total = own_sums[...] + near_sums[...].astype(F32) + far_sums[...].astype(F32)
    grad_keys[0] = total[:, 0:width].astype(BF16)
    grad_values[0] = total[:, width : 2 * width].astype(BF16)


def per_device(queries, keys, values, attn_out, log_sums, grad_held, doc_ids):
    arrived = from_behind(grad_held, "section", -1)
    rows, width = keys.shape[1:]
    docs = doc_ids.reshape(1, rows)
    packed = pl.pallas_call(
        pack_kernel,
        out_shape=jax.ShapeDtypeStruct((rows + DOC_ROWS, 2 * width), BF16),
        in_specs=vmem(3),
        out_specs=pl.BlockSpec(memory_space=pltpu.VMEM),
        name="pack",
    )(keys, values, docs)
    far = shifted(packed, "ctx", 2)
    near = shifted(packed, "ctx", 1)
    place = lax.axis_index("ctx").astype(jnp.int32).reshape(1)
    sums = lambda dtype: jax.ShapeDtypeStruct((rows, 2 * width), dtype)
    dq, own_sums, near_sums, far_sums = pl.pallas_call(
        grads_kernel,
        out_shape=(jax.ShapeDtypeStruct(queries.shape, BF16), sums(F32), sums(BF16), sums(BF16)),
        in_specs=[pl.BlockSpec(memory_space=pltpu.SMEM)] + vmem(8),
        out_specs=tuple(vmem(4)),
        scratch_shapes=[pltpu.VMEM((HOPS + 1, rows, rows), F32)],
        compiler_params=pltpu.CompilerParams(vmem_limit_bytes=32 * 1024 * 1024),
        name="grads",
    )(place, queries, attn_out, arrived, log_sums, docs, packed, near, far)
    near_back = shifted(near_sums, "ctx", -1)
    far_back = shifted(far_sums, "ctx", -2)
    grad_keys, grad_values = pl.pallas_call(
        add_kernel,
        out_shape=(jax.ShapeDtypeStruct(keys.shape, BF16), jax.ShapeDtypeStruct(values.shape, BF16)),
        in_specs=vmem(3),
        out_specs=tuple(vmem(2)),
        name="add",
    )(own_sums, near_back, far_back)
    return dq, grad_keys, grad_values


def solution(mesh):
    placed = (
        P("section", "ctx", None),
        P("section", "ctx", None),
        P("section", "ctx", None),
        P("section", "ctx", None),
        P("section", None, "ctx"),
        P("section", "ctx", None),
        P("ctx"),
    )
    return jax.shard_map(
        per_device,
        mesh=mesh,
        in_specs=placed,
        out_specs=(P("section", "ctx", None), P("section", "ctx", None), P("section", "ctx", None)),
        check_vma=False,
    )
```

time: 62.7 us -> 38.4 us (0.61)
  matrix products: 18.9 us -> 0 us
  starting transfers between devices: 27.4 us -> 10.9 us
  Pallas kernels: 0 us -> 10.1 us
  waiting for transfers between devices: 7.34 us -> 11.6 us
  local copies, waits for them, and re-layouts: 6.29 us -> 4.34 us
  other arithmetic: 0.93 us -> 0 us
    dot_general x15 -> x0, matrix products: 18.9 us -> none  [the longest x3 5.84 us: key_part(): jnp.einsum('hqk,qhd->kd', weights_low, grad_heads, preferred_element_type...]
    ppermute x10 -> x4, starting transfers between devices: 27.4 us -> 10.4 us  [shifted(): return lax.ppermute(array, axis, pairs)]
    pallas_call x0 -> x3, Pallas kernels: none -> 10.1 us  [the longest x1 6.85 us: per_device(): pl.pallas_call(grads_kernel, out_shape=(jax.ShapeDtypeStruct(queries.shap...]
    ppermute x10 -> x4, waiting for transfers between devices: 7.34 us -> 11.6 us  [shifted(): return lax.ppermute(array, axis, pairs)]
    unnamed x35 -> x16, local copies, waits for them, and re-layouts: 6.24 us -> 4.34 us
  transfers between devices with their start and end apart: 11 -> 5, of which waited for: 1 -> 4; matrix products, arithmetic and copies ran while one was open for 40% -> 0% of each run, Pallas kernels for 0% -> 4%
where the time goes in v1:
time: 38.4 us; the launch traced here: 37.7 us
  waiting for transfers between devices  11.6 us (30%)
  starting transfers between devices  10.9 us (28%)
  Pallas kernels  10.1 us (26%)
  local copies, waits for them, and re-layouts  4.34 us (11%)
  between operations  0.69 us (2%)
    ppermute x4, waiting for transfers between devices, shifted(): return lax.ppermute(array, axis, pairs)  11.6 us
    ppermute x4, starting transfers between devices, shifted(): return lax.ppermute(array, axis, pairs)  10.4 us
    pallas_call x1, Pallas kernels, per_device(): pl.pallas_call(grads_kernel, out_shape=(jax.ShapeDtypeStruct(queries.shap...  6.85 us
    unnamed x16, local copies, waits for them, and re-layouts  4.34 us
    pallas_call x1, Pallas kernels, per_device(): pl.pallas_call(add_kernel, out_shape=(jax.ShapeDtypeStruct(keys.shape, BF...  1.72 us
    pallas_call x1, Pallas kernels, per_device(): pl.pallas_call(pack_kernel, out_shape=jax.ShapeDtypeStruct((rows + DOC_RO...  1.57 us
  transfers between devices with their start and end apart: 5, of which 4 were waited for; matrix products, arithmetic and copies ran while one was open for 0% of the time, Pallas kernels for 4%

profile of v1, /device:TPU:0, one launch (start us, length us, event | category | flops | bytes accessed | tf_op | source)
XLA Modules:
  0.0 37.7 jit_solution(3210393567527888431)
XLA Ops:
  0.6 0.5 %collective-permute-start = (bf16[1,256,1024]{2,1,0:T(8,128)(2,1)}, bf16[1,256,1024]{2,1,0:T(8,128)(2,1)S(1)}, u32[]{:S(2)}, u32[]{:S(2)}) collective-permute-start(bf16[1,256,1024]{2,1,0:T(8,128)(2,1)} %param.12), channel_id=1, source_target_pairs={{16,0},{0,16},{17,1},{1,17},{18,2},{2,18},{19,3},{3,19},{20,4},{4,... | collective-permute-start | bytes 1572872 | tf_op jit(solution)/shard_map/ppermute | solution.py:22
  1.1 0.0 copy-start.4
  1.2 1.6 %pack.1.own = bf16[272,256]{1,0:T(8,128)(2,1)} custom-call(bf16[1,256,128]{2,1,0:T(8,128)(2,1)} %keys.1, bf16[1,256,128]{2,1,0:T(8,128)(2,1)} %values.1, s32[1,256]{1,0:T(1,128)} %bitcast.2), custom_call_target="tpu_custom_call" | custom-call | tf_op jit(solution)/shard_map/pack/pallas_call | solution.py:114
  2.7 4.4 %collective-permute-start.2 = (bf16[272,256]{1,0:T(8,128)(2,1)}, bf16[272,256]{1,0:T(8,128)(2,1)S(1)}, u32[]{:S(2)}, u32[]{:S(2)}) collective-permute-start(bf16[272,256]{1,0:T(8,128)(2,1)} %pack.1.own), channel_id=1, source_target_pairs={{0,2},{1,3},{2,4},{3,5},{4,6},{5,7},{6,8},{7,9},{8,10},{9,11},{10,... | collective-permute-start | bytes 417800 | tf_op jit(solution)/shard_map/ppermute | solution.py:28
  7.2 3.4 %collective-permute-start.1 = (bf16[272,256]{1,0:T(8,128)(2,1)}, bf16[272,256]{1,0:T(8,128)(2,1)S(1)}, u32[]{:S(2)}, u32[]{:S(2)}) collective-permute-start(bf16[272,256]{1,0:T(8,128)(2,1)} %pack.1.own), channel_id=1, source_target_pairs={{0,1},{1,2},{2,3},{3,4},{4,5},{5,6},{6,7},{7,8},{8,9},{9,10},{10,1... | collective-permute-start | bytes 417800 | tf_op jit(solution)/shard_map/ppermute | solution.py:28
  10.6 0.0 copy-start.5
  10.6 0.5 %collective-permute-done.2.far = bf16[272,256]{1,0:T(8,128)(2,1)S(1)} collective-permute-done((bf16[272,256]{1,0:T(8,128)(2,1)}, bf16[272,256]{1,0:T(8,128)(2,1)S(1)}, u32[]{:S(2)}, u32[]{:S(2)}) %collective-permute-start.2) | collective-permute-done | bytes 139296 | tf_op jit(solution)/shard_map/ppermute | solution.py:28
  11.0 3.1 %collective-permute-done.1.near = bf16[272,256]{1,0:T(8,128)(2,1)S(1)} collective-permute-done((bf16[272,256]{1,0:T(8,128)(2,1)}, bf16[272,256]{1,0:T(8,128)(2,1)S(1)}, u32[]{:S(2)}, u32[]{:S(2)}) %collective-permute-start.1) | collective-permute-done | bytes 139296 | tf_op jit(solution)/shard_map/ppermute | solution.py:28
  14.2 0.0 collective-permute-done.grads
  14.2 0.0 copy-done.4
  14.2 0.0 copy-done.5
  14.2 0.0 copy-start
  14.2 0.9 %copy-done = bf16[272,256]{1,0:T(8,128)(2,1)S(1)} copy-done((bf16[272,256]{1,0:T(8,128)(2,1)S(1)}, bf16[272,256]{1,0:T(8,128)(2,1)}, u32[]{:S(2)}) %copy-start) | copy-done | bytes 139288
  15.1 0.0 copy-start.1
  15.1 1.0 %copy-done.1 = bf16[1,256,1024]{2,1,0:T(8,128)(2,1)S(1)} copy-done((bf16[1,256,1024]{2,1,0:T(8,128)(2,1)S(1)}, bf16[1,256,1024]{2,1,0:T(8,128)(2,1)}, u32[]{:S(2)}) %copy-start.1) | copy-done | bytes 524312
  16.1 0.0 copy-start.2
  16.1 1.0 %copy-done.2 = bf16[1,256,1024]{2,1,0:T(8,128)(2,1)S(1)} copy-done((bf16[1,256,1024]{2,1,0:T(8,128)(2,1)S(1)}, bf16[1,256,1024]{2,1,0:T(8,128)(2,1)}, u32[]{:S(2)}) %copy-start.2) | copy-done | bytes 524312
  17.2 6.8 %grads.1 = (bf16[1,256,1024]{2,1,0:T(8,128)(2,1)}, f32[256,256]{1,0:T(8,128)S(1)}, bf16[256,256]{1,0:T(8,128)(2,1)S(1)}, bf16[256,256]{1,0:T(8,128)(2,1)S(1)}) custom-call(s32[1]{0:T(128)} %bitcast.place, bf16[1,256,1024]{2,1,0:T(8,128)(2,1)S(1)} %copy-done.1, bf16[1,256,1024]{2,1,0:T(8,128)(2,1)S(1)} %copy-done.2, ...), custom_call_target="tpu_custom_call" | custom-call | tf_op jit(solution)/shard_map/grads/pallas_call | solution.py:125
  24.0 0.0 copy-start.3
  24.0 0.7 %copy-done.3 = f32[256,256]{1,0:T(8,128)} copy-done((f32[256,256]{1,0:T(8,128)}, f32[256,256]{1,0:T(8,128)S(1)}, u32[]{:S(2)}) %copy-start.3) | copy-done | bytes 262168
  24.7 1.3 %collective-permute-start.3 = (bf16[256,256]{1,0:T(8,128)(2,1)S(1)}, bf16[256,256]{1,0:T(8,128)(2,1)S(1)}, u32[]{:S(2)}, u32[]{:S(2)}) collective-permute-start(bf16[256,256]{1,0:T(8,128)(2,1)S(1)} %get-tuple-element.11), channel_id=1, source_target_pairs={{1,0},{2,1},{3,2},{4,3},{5,4},{6,5},{7,6},{8,7},{9,8},{10,9},{11,1... | collective-permute-start | bytes 393224 | tf_op jit(solution)/shard_map/ppermute | solution.py:28
  26.0 1.3 %collective-permute-start.4 = (bf16[256,256]{1,0:T(8,128)(2,1)S(1)}, bf16[256,256]{1,0:T(8,128)(2,1)S(1)}, u32[]{:S(2)}, u32[]{:S(2)}) collective-permute-start(bf16[256,256]{1,0:T(8,128)(2,1)S(1)} %get-tuple-element.12), channel_id=1, source_target_pairs={{2,0},{3,1},{4,2},{5,3},{6,4},{7,5},{8,6},{9,7},{10,8},{11,9},{12,... | collective-permute-start | bytes 393224 | tf_op jit(solution)/shard_map/ppermute | solution.py:28
  27.3 4.7 %collective-permute-done.3.near_sums = bf16[256,256]{1,0:T(8,128)(2,1)S(1)} collective-permute-done((bf16[256,256]{1,0:T(8,128)(2,1)S(1)}, bf16[256,256]{1,0:T(8,128)(2,1)S(1)}, u32[]{:S(2)}, u32[]{:S(2)}) %collective-permute-start.3) | collective-permute-done | bytes 131104 | tf_op jit(solution)/shard_map/ppermute | solution.py:28
  32.1 0.0 copy-start.6
  32.1 3.3 %collective-permute-done.4.far_sums = bf16[256,256]{1,0:T(8,128)(2,1)S(1)} collective-permute-done((bf16[256,256]{1,0:T(8,128)(2,1)S(1)}, bf16[256,256]{1,0:T(8,128)(2,1)S(1)}, u32[]{:S(2)}, u32[]{:S(2)}) %collective-permute-start.4) | collective-permute-done | bytes 131104 | tf_op jit(solution)/shard_map/ppermute | solution.py:28
  35.3 0.0 copy-start.7
  35.3 0.0 copy-done.6
  35.3 0.6 %copy-done.7 = bf16[256,256]{1,0:T(8,128)(2,1)} copy-done((bf16[256,256]{1,0:T(8,128)(2,1)}, bf16[256,256]{1,0:T(8,128)(2,1)S(1)}, u32[]{:S(2)}) %copy-start.7) | copy-done | bytes 131096
  36.0 1.7 %add.1 = (bf16[1,256,128]{2,1,0:T(8,128)(2,1)}, bf16[1,256,128]{2,1,0:T(8,128)(2,1)}) custom-call(f32[256,256]{1,0:T(8,128)} %copy-done.3, bf16[256,256]{1,0:T(8,128)(2,1)} %copy-done.6, bf16[256,256]{1,0:T(8,128)(2,1)} %copy-done.7), custom_call_target="tpu_custom_call" | custom-call | tf_op jit(solution)/shard_map/add/pallas_call | solution.py:136
Async XLA Ops:
  0.6 13.5 %collective-permute-start = (bf16[1,256,1024]{2,1,0:T(8,128)(2,1)}, bf16[1,256,1024]{2,1,0:T(8,128)(2,1)S(1)}, u32[]{:S(2)}, u32[]{:S(2)}) collective-permute-start(bf16[1,256,1024]{2,1,0:T(8,128)(2,1)} %param.12), channel_id=1, source_target_pairs={{16,0},{0,16},{17,1},{1,17},{18,2},{2,18},{19,3},{3,19},{20,4},{4,... | collective-permute-start | bytes 1572872 | tf_op jit(solution)/shard_map/ppermute | solution.py:22
  1.1 13.0 %copy-start.4 = (f32[1,8,256]{2,1,0:T(8,128)S(1)}, f32[1,8,256]{2,1,0:T(8,128)}, u32[]{:S(2)}) copy-start(f32[1,8,256]{2,1,0:T(8,128)} %log_sums.1) | copy-start | bytes 24580
  2.7 8.3 %collective-permute-start.2 = (bf16[272,256]{1,0:T(8,128)(2,1)}, bf16[272,256]{1,0:T(8,128)(2,1)S(1)}, u32[]{:S(2)}, u32[]{:S(2)}) collective-permute-start(bf16[272,256]{1,0:T(8,128)(2,1)} %pack.1.own), channel_id=1, source_target_pairs={{0,2},{1,3},{2,4},{3,5},{4,6},{5,7},{6,8},{7,9},{8,10},{9,11},{10,... | collective-permute-start | bytes 417800 | tf_op jit(solution)/shard_map/ppermute | solution.py:28
  7.2 7.0 %collective-permute-start.1 = (bf16[272,256]{1,0:T(8,128)(2,1)}, bf16[272,256]{1,0:T(8,128)(2,1)S(1)}, u32[]{:S(2)}, u32[]{:S(2)}) collective-permute-start(bf16[272,256]{1,0:T(8,128)(2,1)} %pack.1.own), channel_id=1, source_target_pairs={{0,1},{1,2},{2,3},{3,4},{4,5},{5,6},{6,7},{7,8},{8,9},{9,10},{10,1... | collective-permute-start | bytes 417800 | tf_op jit(solution)/shard_map/ppermute | solution.py:28
  10.6 3.6 %copy-start.5 = (s32[256]{0:T(256)S(1)}, s32[256]{0:T(256)}, u32[]{:S(2)}) copy-start(s32[256]{0:T(256)} %param.13) | copy-start | bytes 3076
  14.2 0.9 %copy-start = (bf16[272,256]{1,0:T(8,128)(2,1)S(1)}, bf16[272,256]{1,0:T(8,128)(2,1)}, u32[]{:S(2)}) copy-start(bf16[272,256]{1,0:T(8,128)(2,1)} %pack.1.own) | copy-start | bytes 417796
  15.1 1.0 %copy-start.1 = (bf16[1,256,1024]{2,1,0:T(8,128)(2,1)S(1)}, bf16[1,256,1024]{2,1,0:T(8,128)(2,1)}, u32[]{:S(2)}) copy-start(bf16[1,256,1024]{2,1,0:T(8,128)(2,1)} %queries.1) | copy-start | bytes 1572868
  16.1 1.0 %copy-start.2 = (bf16[1,256,1024]{2,1,0:T(8,128)(2,1)S(1)}, bf16[1,256,1024]{2,1,0:T(8,128)(2,1)}, u32[]{:S(2)}) copy-start(bf16[1,256,1024]{2,1,0:T(8,128)(2,1)} %attn_out.1) | copy-start | bytes 1572868
  24.0 0.7 %copy-start.3 = (f32[256,256]{1,0:T(8,128)}, f32[256,256]{1,0:T(8,128)S(1)}, u32[]{:S(2)}) copy-start(f32[256,256]{1,0:T(8,128)S(1)} %get-tuple-element.10.own_sums) | copy-start | bytes 786436
  24.7 7.3 %collective-permute-start.3 = (bf16[256,256]{1,0:T(8,128)(2,1)S(1)}, bf16[256,256]{1,0:T(8,128)(2,1)S(1)}, u32[]{:S(2)}, u32[]{:S(2)}) collective-permute-start(bf16[256,256]{1,0:T(8,128)(2,1)S(1)} %get-tuple-element.11), channel_id=1, source_target_pairs={{1,0},{2,1},{3,2},{4,3},{5,4},{6,5},{7,6},{8,7},{9,8},{10,9},{11,1... | collective-permute-start | bytes 393224 | tf_op jit(solution)/shard_map/ppermute | solution.py:28
  26.0 9.3 %collective-permute-start.4 = (bf16[256,256]{1,0:T(8,128)(2,1)S(1)}, bf16[256,256]{1,0:T(8,128)(2,1)S(1)}, u32[]{:S(2)}, u32[]{:S(2)}) collective-permute-start(bf16[256,256]{1,0:T(8,128)(2,1)S(1)} %get-tuple-element.12), channel_id=1, source_target_pairs={{2,0},{3,1},{4,2},{5,3},{6,4},{7,5},{8,6},{9,7},{10,8},{11,9},{12,... | collective-permute-start | bytes 393224 | tf_op jit(solution)/shard_map/ppermute | solution.py:28
  32.1 3.3 %copy-start.6 = (bf16[256,256]{1,0:T(8,128)(2,1)}, bf16[256,256]{1,0:T(8,128)(2,1)S(1)}, u32[]{:S(2)}) copy-start(bf16[256,256]{1,0:T(8,128)(2,1)S(1)} %collective-permute-done.3.near_sums) | copy-start | bytes 393220
  35.3 0.6 %copy-start.7 = (bf16[256,256]{1,0:T(8,128)(2,1)}, bf16[256,256]{1,0:T(8,128)(2,1)S(1)}, u32[]{:S(2)}) copy-start(bf16[256,256]{1,0:T(8,128)(2,1)S(1)} %collective-permute-done.4.far_sums) | copy-start | bytes 393220

commit v2 on v1

v2 whole, which is shorter than its diff:
```python
import jax
import jax.numpy as jnp
from jax import lax
from jax.experimental import pallas as pl
from jax.experimental.pallas import tpu as pltpu
from jax.sharding import PartitionSpec as P

HOPS = 2
DOC_ROWS = 16
LOG2_E = 1.4426950408889634
MASKED = -1e30

F32 = jnp.float32
BF16 = jnp.bfloat16


def from_behind(block, axis, distance):
    devices = range(lax.axis_size(axis))
    route = [((i - distance) % len(devices), i) for i in devices]
    return lax.ppermute(block, axis, route)


def shifted(array, axis, by):
    devices = lax.axis_size(axis)
    pairs = [(i, i + by) for i in range(devices) if 0 <= i + by < devices]
    return lax.ppermute(array, axis, pairs)


def dot_nt(a, b):
    return lax.dot_general(a, b, (((1,), (1,)), ((), ())), preferred_element_type=F32)


def dot_nn(a, b):
    return lax.dot_general(a, b, (((1,), (0,)), ((), ())), preferred_element_type=F32)


def vmem(count):
    return [pl.BlockSpec(memory_space=pltpu.VMEM)] * count


def pack_kernel(keys, values, docs, packed, docs_here, sems):
    rows, width = keys.shape[1:]
    copies = [
        pltpu.make_async_copy(docs, docs_here, sems.at[0]),
        pltpu.make_async_copy(keys.at[0], packed.at[0:rows, 0:width], sems.at[1]),
        pltpu.make_async_copy(values.at[0], packed.at[0:rows, width : 2 * width], sems.at[2]),
    ]
    for copy in copies:
        copy.start()
    copies[0].wait()
    docs_row = (docs_here[...] + 1).astype(F32).astype(BF16)
    packed[rows : rows + DOC_ROWS, :] = jnp.broadcast_to(docs_row, (DOC_ROWS, docs_row.shape[1]))
    for copy in copies[1:]:
        copy.wait()


def column_of(row, width):
    rows = row.shape[1]
    column = jnp.transpose(jnp.broadcast_to(row, (width, rows)))
    return jnp.concatenate([column] * (rows // width), axis=1)


def block_grads(queries, grads, log_sums, delta_of, block, bias, score_grads, sums):
    rows = queries.shape[1]
    heads = log_sums.shape[1]
    width = queries.shape[2] // heads
    scale = float(width) ** -0.5
    sum_k = sum_v = None
    for head in range(heads):
        part = slice(head * width, (head + 1) * width)
        g = grads[0, :, part]
        delta = delta_of(head, part, g)
        q = queries[0, :, part]
        lse = log_sums[0, head : head + 1, :] * LOG2_E
        scores = dot_nt(block[0:rows, 0:width], q)
        weights = jnp.exp2(scores * (scale * LOG2_E) - lse + bias[...])
        weight_grads = dot_nt(block[0:rows, width : 2 * width], g)
        low = (weights * (weight_grads - delta)).astype(BF16)
        score_grads[head] = low
        term_v = dot_nn(weights.astype(BF16), g)
        term_k = dot_nn(low, q)
        sum_v = term_v if head == 0 else sum_v + term_v
        sum_k = term_k if head == 0 else sum_k + term_k
    sums[:, 0:width] = (sum_k * scale).astype(sums.dtype)
    sums[:, width : 2 * width] = sum_v.astype(sums.dtype)


def own_kernel(queries, attn_out, grads, log_sums, block, score_grads, sums, deltas, bias):
    rows = queries.shape[1]
    width = block.shape[1] // 2
    docs = block[rows : rows + DOC_ROWS, :].astype(F32)[0:1]
    key_at = lax.broadcasted_iota(jnp.int32, (rows, rows), 0)
    query_at = lax.broadcasted_iota(jnp.int32, (rows, rows), 1)
    bias[...] = jnp.where((column_of(docs, width) == docs) & (key_at <= query_at), 0.0, MASKED)
    one = jnp.ones((8, width), BF16)

    def delta_of(head, part, g):
        product = g.astype(F32) * attn_out[0, :, part].astype(F32)
        high = product.astype(BF16)
        low = (product - high.astype(F32)).astype(BF16)
        delta = (dot_nt(one, high) + dot_nt(one, low))[0:1]
        deltas[head : head + 1, :] = delta
        return delta

    block_grads(queries, grads, log_sums, delta_of, block, bias, score_grads, sums)


def hop_kernel(queries, grads, log_sums, deltas, own, block, before, score_grads, sums, bias):
    rows = queries.shape[1]
    width = block.shape[1] // 2
    docs = own[rows : rows + DOC_ROWS, :].astype(F32)[0:1]
    far_docs = block[rows : rows + DOC_ROWS, :].astype(F32)[0:1]
    bias[...] = jnp.where(column_of(far_docs, width) == docs, 0.0, MASKED)
    delta_of = lambda head, part, g: deltas[head : head + 1, :]
    block_grads(queries, grads, log_sums, delta_of, block, bias, score_grads, sums)


def query_kernel(own, near, far, own_grads, near_grads, far_grads, grad_queries):
    heads, rows = own_grads.shape[0:2]
    width = own.shape[1] // 2
    scale = float(width) ** -0.5
    turned = [jnp.transpose(block[0:rows, 0:width].astype(F32)).astype(BF16) for block in (own, near, far)]
    for head in range(heads):
        total = dot_nn(turned[0], own_grads[head]) + dot_nn(turned[1], near_grads[head]) + dot_nn(turned[2], far_grads[head])
        grad_queries[0, :, head * width : (head + 1) * width] = jnp.transpose(total * scale).astype(BF16)


def add_kernel(own_sums, near_sums, far_sums, grad_keys, grad_values):
    width = grad_keys.shape[2]
    total = own_sums[...] + near_sums[...].astype(F32) + far_sums[...].astype(F32)
    grad_keys[0] = total[:, 0:width].astype(BF16)
    grad_values[0] = total[:, width : 2 * width].astype(BF16)


def call(kernel, name, outs, args, flops=0, scratch=(), from_hbm=0, limit=8):
    args = [pltpu.with_memory_space_constraint(a, pltpu.HBM) for a in args[:from_hbm]] + list(args[from_hbm:])
    moved = sum(a.size * a.dtype.itemsize for a in args)
    return pl.pallas_call(
        kernel,
        out_shape=outs,
        in_specs=[pl.BlockSpec(memory_space=pltpu.HBM)] * from_hbm + vmem(len(args) - from_hbm),
        out_specs=tuple(vmem(len(outs))),
        scratch_shapes=list(scratch),
        compiler_params=pltpu.CompilerParams(vmem_limit_bytes=limit * 1024 * 1024),
        cost_estimate=pl.CostEstimate(flops=flops, bytes_accessed=moved, transcendentals=0),
        name=name,
    )(*args)


def per_device(queries, keys, values, attn_out, log_sums, grad_held, doc_ids):
    rows, width = keys.shape[1:]
    heads = log_sums.shape[1]
    shape = jax.ShapeDtypeStruct
    flops = 2 * heads * rows * rows * width
    bias = pltpu.VMEM((rows, rows), F32)
    score_grads = shape((heads, rows, rows), BF16)
    sums = lambda dtype: shape((rows, 2 * width), dtype)

    grads = from_behind(grad_held, "section", -1)
    (own,) = call(
        pack_kernel,
        "pack",
        (shape((rows + DOC_ROWS, 2 * width), BF16),),
        (keys, values, doc_ids.reshape(1, rows)),
        40 * flops,
        [pltpu.VMEM((1, rows), jnp.int32), pltpu.SemaphoreType.DMA((3,))],
        3,
    )
    near = shifted(own, "ctx", 1)
    far = shifted(own, "ctx", 2)
    own_grads, own_sums, deltas = call(
        own_kernel, "own_block", (score_grads, sums(F32), shape((heads, rows), F32)), (queries, attn_out, grads, log_sums, own), 4 * flops, [bias]
    )
    hop = lambda name, block, before: call(hop_kernel, name, (score_grads, sums(BF16)), (queries, grads, log_sums, deltas, own, block, before), 4 * flops, [bias])
    near_grads, near_sums = hop("near_block", near, own_sums)
    near_back = shifted(near_sums, "ctx", -1)
    far_grads, far_sums = hop("far_block", far, near_sums)
    far_back = shifted(far_sums, "ctx", -2)
    (grad_queries,) = call(query_kernel, "query_grads", (shape(queries.shape, BF16),), (own, near, far, own_grads, near_grads, far_grads), 3 * flops)
    grad_keys, grad_values = call(add_kernel, "add", (shape(keys.shape, BF16), shape(values.shape, BF16)), (own_sums, near_back, far_back))
    return grad_queries, grad_keys, grad_values


def solution(mesh):
    placed = (
        P("section", "ctx", None),
        P("section", "ctx", None),
        P("section", "ctx", None),
        P("section", "ctx", None),
        P("section", None, "ctx"),
        P("section", "ctx", None),
        P("ctx"),
    )
    return jax.shard_map(
        per_device,
        mesh=mesh,
        in_specs=placed,
        out_specs=(P("section", "ctx", None), P("section", "ctx", None), P("section", "ctx", None)),
        check_vma=False,
    )
```

time: 38.4 us -> 26.9 us (0.70); the launches traced: 37.7 us -> 26.7 us
  waiting for transfers between devices: 11.6 us -> 5.98 us
  local copies, waits for them, and re-layouts: 4.34 us -> 0.01 us
  Pallas kernels: 10.1 us -> 9.04 us
    ppermute x4, waiting for transfers between devices: 11.6 us -> 5.98 us  [shifted(): return lax.ppermute(array, axis, pairs)]
    unnamed x16 -> x6, local copies, waits for them, and re-layouts: 4.34 us -> 0.01 us
    pallas_call x3 -> x6, Pallas kernels: 10.1 us -> 9.04 us  [call(): pl.pallas_call(kernel, out_shape=outs, in_specs=[pl.BlockSpec(memory_spac...]
  transfers between devices with their start and end apart: 5 -> 5, of which waited for: 4 -> 2; matrix products, arithmetic and copies ran while one was open for 0% -> 0% of each run, Pallas kernels for 4% -> 31%
where the time goes in v2:
time: 26.9 us; the launch traced here: 26.7 us
  starting transfers between devices  11 us (41%)
  Pallas kernels  9.04 us (34%)
  waiting for transfers between devices  5.98 us (22%)
  between operations  0.74 us (3%)
    ppermute x4, starting transfers between devices, shifted(): return lax.ppermute(array, axis, pairs)  10.4 us
    pallas_call x6, Pallas kernels, call(): pl.pallas_call(kernel, out_shape=outs, in_specs=[pl.BlockSpec(memory_spac...  9.04 us
    ppermute x4, waiting for transfers between devices, shifted(): return lax.ppermute(array, axis, pairs)  5.98 us
  transfers between devices with their start and end apart: 5, of which 2 were waited for; matrix products, arithmetic and copies ran while one was open for 0% of the time, Pallas kernels for 31%

profile of v2, /device:TPU:0, one launch (start us, length us, event | category | flops | bytes accessed | tf_op | source)
XLA Modules:
  0.0 26.7 jit_solution(8598952860171242288)
XLA Ops:
  0.6 0.5 %collective-permute-start.2 = (bf16[1,256,1024]{2,1,0:T(8,128)(2,1)}, bf16[1,256,1024]{2,1,0:T(8,128)(2,1)S(1)}, u32[]{:S(2)}, u32[]{:S(2)}) collective-permute-start(bf16[1,256,1024]{2,1,0:T(8,128)(2,1)} %param.12), channel_id=1, source_target_pairs={{16,0},{0,16},{17,1},{1,17},{18,2},{2,18},{19,3},{3,19},{20,4},{4,... | collective-permute-start | bytes 1572872 | tf_op jit(solution)/shard_map/ppermute | solution.py:20
  1.2 0.0 copy-start
  1.2 0.0 copy-start.1
  1.2 0.0 copy-start.2
  1.2 1.0 %pack.1.block.own = bf16[272,256]{1,0:T(8,128)(2,1)S(1)} custom-call(bf16[1,256,128]{2,1,0:T(8,128)(2,1)} %keys.1, bf16[1,256,128]{2,1,0:T(8,128)(2,1)} %values.1, s32[1,256]{1,0:T(1,128)} %bitcast.1), custom_call_target="tpu_custom_call" | custom-call | flops 5368709120 | bytes 132096 | tf_op jit(solution)/shard_map/pack/pallas_call | solution.py:138
  2.2 4.4 %collective-permute-start = (bf16[272,256]{1,0:T(8,128)(2,1)S(1)}, bf16[272,256]{1,0:T(8,128)(2,1)S(1)}, u32[]{:S(2)}, u32[]{:S(2)}) collective-permute-start(bf16[272,256]{1,0:T(8,128)(2,1)S(1)} %pack.1.block.own), channel_id=1, source_target_pairs={{0,1},{1,2},{2,3},{3,4},{4,5},{5,6},{6,7},{7,8},{8,9},{9,10},{10,1... | collective-permute-start | bytes 417800 | tf_op jit(solution)/shard_map/ppermute | solution.py:26
  6.6 3.4 %collective-permute-start.1 = (bf16[272,256]{1,0:T(8,128)(2,1)S(1)}, bf16[272,256]{1,0:T(8,128)(2,1)S(1)}, u32[]{:S(2)}, u32[]{:S(2)}) collective-permute-start(bf16[272,256]{1,0:T(8,128)(2,1)S(1)} %pack.1.block.own), channel_id=1, source_target_pairs={{0,2},{1,3},{2,4},{3,5},{4,6},{5,7},{6,8},{7,9},{8,10},{9,11},{10,... | collective-permute-start | bytes 417800 | tf_op jit(solution)/shard_map/ppermute | solution.py:26
  10.0 0.0 collective-permute-done.2.grads
  10.1 0.0 copy-done
  10.1 0.0 copy-done.1
  10.1 0.0 copy-done.2
  10.1 2.1 %own_block.1 = (bf16[8,256,256]{2,1,0:T(8,128)(2,1)S(1)}, f32[256,256]{1,0:T(8,128)S(1)}, f32[8,256]{1,0:T(8,128)S(1)}) custom-call(bf16[1,256,1024]{2,1,0:T(8,128)(2,1)S(1)} %copy-done.1, bf16[1,256,1024]{2,1,0:T(8,128)(2,1)S(1)} %copy-done, bf16[1,256,1024]{2,1,0:T(8,128)(2,1)S(1)} %collective-permute-done.2.grads, f32[1,8,256]{2,1,0:T(8,128)S(1)} %copy-done.2, ...), custom_call_target="tpu_custom_call" | custom-call | flops 536870912 | bytes 1720320 | tf_op jit(solution)/shard_map/own_block/pallas_call | solution.py:138
  12.2 0.0 collective-permute-done.block.near
  12.2 1.9 %near_block.1 = (bf16[8,256,256]{2,1,0:T(8,128)(2,1)S(1)}, bf16[256,256]{1,0:T(8,128)(2,1)S(1)}) custom-call(bf16[1,256,1024]{2,1,0:T(8,128)(2,1)S(1)} %copy-done.1, bf16[1,256,1024]{2,1,0:T(8,128)(2,1)S(1)} %collective-permute-done.2.grads, f32[1,8,256]{2,1,0:T(8,128)S(1)} %copy-done.2, f32[8,256]{1,0:T(8,128)S(1)} %get-tuple-element.13.deltas, ...), custom_call_target="tpu_custom_call" | custom-call | flops 536870912 | bytes 1605632 | tf_op jit(solution)/shard_map/near_block/pallas_call | solution.py:138
  14.1 1.3 %collective-permute-start.3 = (bf16[256,256]{1,0:T(8,128)(2,1)S(1)}, bf16[256,256]{1,0:T(8,128)(2,1)S(1)}, u32[]{:S(2)}, u32[]{:S(2)}) collective-permute-start(bf16[256,256]{1,0:T(8,128)(2,1)S(1)} %get-tuple-element.16.before), channel_id=1, source_target_pairs={{1,0},{2,1},{3,2},{4,3},{5,4},{6,5},{7,6},{8,7},{9,8},{10,9},{11,1... | collective-permute-start | bytes 393224 | tf_op jit(solution)/shard_map/ppermute | solution.py:26
  15.4 0.0 collective-permute-done.1.block.far
  15.4 1.9 %far_block.1 = (bf16[8,256,256]{2,1,0:T(8,128)(2,1)S(1)}, bf16[256,256]{1,0:T(8,128)(2,1)S(1)}) custom-call(bf16[1,256,1024]{2,1,0:T(8,128)(2,1)S(1)} %copy-done.1, bf16[1,256,1024]{2,1,0:T(8,128)(2,1)S(1)} %collective-permute-done.2.grads, f32[1,8,256]{2,1,0:T(8,128)S(1)} %copy-done.2, f32[8,256]{1,0:T(8,128)S(1)} %get-tuple-element.13.deltas, ...), custom_call_target="tpu_custom_call" | custom-call | flops 536870912 | bytes 1474560 | tf_op jit(solution)/shard_map/far_block/pallas_call | solution.py:138
  17.3 1.3 %collective-permute-start.4 = (bf16[256,256]{1,0:T(8,128)(2,1)S(1)}, bf16[256,256]{1,0:T(8,128)(2,1)S(1)}, u32[]{:S(2)}, u32[]{:S(2)}) collective-permute-start(bf16[256,256]{1,0:T(8,128)(2,1)S(1)} %get-tuple-element.18), channel_id=1, source_target_pairs={{2,0},{3,1},{4,2},{5,3},{6,4},{7,5},{8,6},{9,7},{10,8},{11,9},{12,... | collective-permute-start | bytes 393224 | tf_op jit(solution)/shard_map/ppermute | solution.py:26
  18.6 1.5 %query_grads.1 = bf16[1,256,1024]{2,1,0:T(8,128)(2,1)} custom-call(bf16[272,256]{1,0:T(8,128)(2,1)S(1)} %pack.1.block.own, bf16[272,256]{1,0:T(8,128)(2,1)S(1)} %collective-permute-done.block.near, bf16[272,256]{1,0:T(8,128)(2,1)S(1)} %collective-permute-done.1.block.far, bf16[8,256,256]{2,1,0:T(8,128)(2,1)S(1)} %get-tuple-element.12.own_grads, ...), custom_call_target="tpu_custom_call" | custom-call | flops 402653184 | bytes 3563520 | tf_op jit(solution)/shard_map/query_grads/pallas_call | solution.py:138
  20.1 1.2 %collective-permute-done.3.near_sums = bf16[256,256]{1,0:T(8,128)(2,1)S(1)} collective-permute-done((bf16[256,256]{1,0:T(8,128)(2,1)S(1)}, bf16[256,256]{1,0:T(8,128)(2,1)S(1)}, u32[]{:S(2)}, u32[]{:S(2)}) %collective-permute-start.3) | collective-permute-done | bytes 131104 | tf_op jit(solution)/shard_map/ppermute | solution.py:26
  21.3 4.8 %collective-permute-done.4.far_sums = bf16[256,256]{1,0:T(8,128)(2,1)S(1)} collective-permute-done((bf16[256,256]{1,0:T(8,128)(2,1)S(1)}, bf16[256,256]{1,0:T(8,128)(2,1)S(1)}, u32[]{:S(2)}, u32[]{:S(2)}) %collective-permute-start.4) | collective-permute-done | bytes 131104 | tf_op jit(solution)/shard_map/ppermute | solution.py:26
  26.1 0.7 %add.1 = (bf16[1,256,128]{2,1,0:T(8,128)(2,1)}, bf16[1,256,128]{2,1,0:T(8,128)(2,1)}) custom-call(f32[256,256]{1,0:T(8,128)S(1)} %get-tuple-element.14.before.own_sums, bf16[256,256]{1,0:T(8,128)(2,1)S(1)} %collective-permute-done.3.near_sums, bf16[256,256]{1,0:T(8,128)(2,1)S(1)} %collective-permute-done.4.far_sums), custom_call_target="tpu_custom_call" | custom-call | bytes 524288 | tf_op jit(solution)/shard_map/add/pallas_call | solution.py:138
Async XLA Ops:
  0.6 9.4 %collective-permute-start.2 = (bf16[1,256,1024]{2,1,0:T(8,128)(2,1)}, bf16[1,256,1024]{2,1,0:T(8,128)(2,1)S(1)}, u32[]{:S(2)}, u32[]{:S(2)}) collective-permute-start(bf16[1,256,1024]{2,1,0:T(8,128)(2,1)} %param.12), channel_id=1, source_target_pairs={{16,0},{0,16},{17,1},{1,17},{18,2},{2,18},{19,3},{3,19},{20,4},{4,... | collective-permute-start | bytes 1572872 | tf_op jit(solution)/shard_map/ppermute | solution.py:20
  1.2 8.9 %copy-start = (bf16[1,256,1024]{2,1,0:T(8,128)(2,1)S(1)}, bf16[1,256,1024]{2,1,0:T(8,128)(2,1)}, u32[]{:S(2)}) copy-start(bf16[1,256,1024]{2,1,0:T(8,128)(2,1)} %attn_out.1) | copy-start | bytes 1572868
  1.2 8.9 %copy-start.1 = (bf16[1,256,1024]{2,1,0:T(8,128)(2,1)S(1)}, bf16[1,256,1024]{2,1,0:T(8,128)(2,1)}, u32[]{:S(2)}) copy-start(bf16[1,256,1024]{2,1,0:T(8,128)(2,1)} %queries.5) | copy-start | bytes 1572868
  1.2 8.9 %copy-start.2 = (f32[1,8,256]{2,1,0:T(8,128)S(1)}, f32[1,8,256]{2,1,0:T(8,128)}, u32[]{:S(2)}) copy-start(f32[1,8,256]{2,1,0:T(8,128)} %log_sums.5) | copy-start | bytes 24580
  2.2 10.0 %collective-permute-start = (bf16[272,256]{1,0:T(8,128)(2,1)S(1)}, bf16[272,256]{1,0:T(8,128)(2,1)S(1)}, u32[]{:S(2)}, u32[]{:S(2)}) collective-permute-start(bf16[272,256]{1,0:T(8,128)(2,1)S(1)} %pack.1.block.own), channel_id=1, source_target_pairs={{0,1},{1,2},{2,3},{3,4},{4,5},{5,6},{6,7},{7,8},{8,9},{9,10},{10,1... | collective-permute-start | bytes 417800 | tf_op jit(solution)/shard_map/ppermute | solution.py:26
  6.6 8.8 %collective-permute-start.1 = (bf16[272,256]{1,0:T(8,128)(2,1)S(1)}, bf16[272,256]{1,0:T(8,128)(2,1)S(1)}, u32[]{:S(2)}, u32[]{:S(2)}) collective-permute-start(bf16[272,256]{1,0:T(8,128)(2,1)S(1)} %pack.1.block.own), channel_id=1, source_target_pairs={{0,2},{1,3},{2,4},{3,5},{4,6},{5,7},{6,8},{7,9},{8,10},{9,11},{10,... | collective-permute-start | bytes 417800 | tf_op jit(solution)/shard_map/ppermute | solution.py:26
  14.1 7.2 %collective-permute-start.3 = (bf16[256,256]{1,0:T(8,128)(2,1)S(1)}, bf16[256,256]{1,0:T(8,128)(2,1)S(1)}, u32[]{:S(2)}, u32[]{:S(2)}) collective-permute-start(bf16[256,256]{1,0:T(8,128)(2,1)S(1)} %get-tuple-element.16.before), channel_id=1, source_target_pairs={{1,0},{2,1},{3,2},{4,3},{5,4},{6,5},{7,6},{8,7},{9,8},{10,9},{11,1... | collective-permute-start | bytes 393224 | tf_op jit(solution)/shard_map/ppermute | solution.py:26
  17.3 8.8 %collective-permute-start.4 = (bf16[256,256]{1,0:T(8,128)(2,1)S(1)}, bf16[256,256]{1,0:T(8,128)(2,1)S(1)}, u32[]{:S(2)}, u32[]{:S(2)}) collective-permute-start(bf16[256,256]{1,0:T(8,128)(2,1)S(1)} %get-tuple-element.18), channel_id=1, source_target_pairs={{2,0},{3,1},{4,2},{5,3},{6,4},{7,5},{8,6},{9,7},{10,8},{11,9},{12,... | collective-permute-start | bytes 393224 | tf_op jit(solution)/shard_map/ppermute | solution.py:26

commit v3 on v2

--- a/solution.py
+++ b/solution.py
@@ -60,34 +60,31 @@
     return jnp.concatenate([column] * (rows // width), axis=1)
 
 
-def block_grads(queries, grads, log_sums, delta_of, block, bias, score_grads, sums):
+def block_grads(queries, grads, log_sums, delta_of, block, bias, score_grads, weights_low, sums):
     rows = queries.shape[1]
     heads = log_sums.shape[1]
     width = queries.shape[2] // heads
     scale = float(width) ** -0.5
-    sum_k = sum_v = None
-    for head in range(heads):
-        part = slice(head * width, (head + 1) * width)
+    parts = [slice(head * width, (head + 1) * width) for head in range(heads)]
+    for head, part in enumerate(parts):
+        columns = slice(head * rows, (head + 1) * rows)
         g = grads[0, :, part]
         delta = delta_of(head, part, g)
-        q = queries[0, :, part]
         lse = log_sums[0, head : head + 1, :] * LOG2_E
-        scores = dot_nt(block[0:rows, 0:width], q)
+        scores = dot_nt(block[0:rows, 0:width], queries[0, :, part])
         weights = jnp.exp2(scores * (scale * LOG2_E) - lse + bias[...])
         weight_grads = dot_nt(block[0:rows, width : 2 * width], g)
-        low = (weights * (weight_grads - delta)).astype(BF16)
-        score_grads[head] = low
-        term_v = dot_nn(weights.astype(BF16), g)
-        term_k = dot_nn(low, q)
-        sum_v = term_v if head == 0 else sum_v + term_v
-        sum_k = term_k if head == 0 else sum_k + term_k
-    sums[:, 0:width] = (sum_k * scale).astype(sums.dtype)
-    sums[:, width : 2 * width] = sum_v.astype(sums.dtype)
-
-
-def own_kernel(queries, attn_out, grads, log_sums, block, score_grads, sums, deltas, bias):
+        score_grads[:, columns] = (weights * (weight_grads - delta)).astype(BF16)
+        weights_low[:, columns] = weights.astype(BF16)
+    stacked = lambda ref: jnp.concatenate([ref[0, :, part] for part in parts], axis=0)
+    sums[:, 0:width] = (dot_nn(score_grads[...], stacked(queries)) * scale).astype(sums.dtype)
+    sums[:, width : 2 * width] = dot_nn(weights_low[...], stacked(grads)).astype(sums.dtype)
+
+
+def own_kernel(queries, attn_out, grads, log_sums, block, score_grads, sums, deltas, block_again, bias, weights_low):
     rows = queries.shape[1]
     width = block.shape[1] // 2
+    block_again[...] = block[...]
     docs = block[rows : rows + DOC_ROWS, :].astype(F32)[0:1]
     key_at = lax.broadcasted_iota(jnp.int32, (rows, rows), 0)
     query_at = lax.broadcasted_iota(jnp.int32, (rows, rows), 1)
@@ -102,26 +99,28 @@
         deltas[head : head + 1, :] = delta
         return delta
 
-    block_grads(queries, grads, log_sums, delta_of, block, bias, score_grads, sums)
-
-
-def hop_kernel(queries, grads, log_sums, deltas, own, block, before, score_grads, sums, bias):
+    block_grads(queries, grads, log_sums, delta_of, block, bias, score_grads, weights_low, sums)
+
+
+def hop_kernel(queries, grads, log_sums, deltas, own, block, before, score_grads, sums, bias, weights_low):
     rows = queries.shape[1]
     width = block.shape[1] // 2
     docs = own[rows : rows + DOC_ROWS, :].astype(F32)[0:1]
     far_docs = block[rows : rows + DOC_ROWS, :].astype(F32)[0:1]
     bias[...] = jnp.where(column_of(far_docs, width) == docs, 0.0, MASKED)
     delta_of = lambda head, part, g: deltas[head : head + 1, :]
-    block_grads(queries, grads, log_sums, delta_of, block, bias, score_grads, sums)
+    block_grads(queries, grads, log_sums, delta_of, block, bias, score_grads, weights_low, sums)
 
 
 def query_kernel(own, near, far, own_grads, near_grads, far_grads, grad_queries):
-    heads, rows = own_grads.shape[0:2]
+    rows = own_grads.shape[0]
+    heads = own_grads.shape[1] // rows
     width = own.shape[1] // 2
     scale = float(width) ** -0.5
     turned = [jnp.transpose(block[0:rows, 0:width].astype(F32)).astype(BF16) for block in (own, near, far)]
     for head in range(heads):
-        total = dot_nn(turned[0], own_grads[head]) + dot_nn(turned[1], near_grads[head]) + dot_nn(turned[2], far_grads[head])
+        columns = slice(head * rows, (head + 1) * rows)
+        total = dot_nn(turned[0], own_grads[:, columns]) + dot_nn(turned[1], near_grads[:, columns]) + dot_nn(turned[2], far_grads[:, columns])
         grad_queries[0, :, head * width : (head + 1) * width] = jnp.transpose(total * scale).astype(BF16)
 
 
@@ -152,8 +151,8 @@
     heads = log_sums.shape[1]
     shape = jax.ShapeDtypeStruct
     flops = 2 * heads * rows * rows * width
-    bias = pltpu.VMEM((rows, rows), F32)
-    score_grads = shape((heads, rows, rows), BF16)
+    score_grads = shape((rows, heads * rows), BF16)
+    scratch = [pltpu.VMEM((rows, rows), F32), pltpu.VMEM((rows, heads * rows), BF16)]
     sums = lambda dtype: shape((rows, 2 * width), dtype)
 
     grads = from_behind(grad_held, "section", -1)
@@ -167,11 +166,16 @@
         3,
     )
     near = shifted(own, "ctx", 1)
-    far = shifted(own, "ctx", 2)
-    own_grads, own_sums, deltas = call(
-        own_kernel, "own_block", (score_grads, sums(F32), shape((heads, rows), F32)), (queries, attn_out, grads, log_sums, own), 4 * flops, [bias]
-    )
-    hop = lambda name, block, before: call(hop_kernel, name, (score_grads, sums(BF16)), (queries, grads, log_sums, deltas, own, block, before), 4 * flops, [bias])
+    own_grads, own_sums, deltas, own_again = call(
+        own_kernel,
+        "own_block",
+        (score_grads, sums(F32), shape((heads, rows), F32), shape(own.shape, BF16)),
+        (queries, attn_out, grads, log_sums, own),
+        4 * flops,
+        scratch,
+    )
+    far = shifted(own_again, "ctx", 2)
+    hop = lambda name, block, before: call(hop_kernel, name, (score_grads, sums(BF16)), (queries, grads, log_sums, deltas, own, block, before), 4 * flops, scratch)
     near_grads, near_sums = hop("near_block", near, own_sums)
     near_back = shifted(near_sums, "ctx", -1)
     far_grads, far_sums = hop("far_block", far, near_sums)

time: 26.9 us -> 25.4 us (0.944)
  Pallas kernels: 9.04 us -> 7.5 us
    pallas_call x6, Pallas kernels: 9.04 us -> 7.5 us  [call(): pl.pallas_call(kernel, out_shape=outs, in_specs=[pl.BlockSpec(memory_spac...]
  transfers between devices with their start and end apart: 5 -> 5, of which waited for: 2 -> 3; matrix products, arithmetic and copies ran while one was open for 0% -> 0% of each run, Pallas kernels for 31% -> 27%
where the time goes in v3:
time: 25.4 us; the launch traced here: 25.2 us
  starting transfers between devices  11 us (43%)
  Pallas kernels  7.5 us (30%)
  waiting for transfers between devices  5.98 us (24%)
  between operations  0.73 us (3%)
    ppermute x4, starting transfers between devices, shifted(): return lax.ppermute(array, axis, pairs)  10.4 us
    pallas_call x6, Pallas kernels, call(): pl.pallas_call(kernel, out_shape=outs, in_specs=[pl.BlockSpec(memory_spac...  7.5 us
    ppermute x4, waiting for transfers between devices, shifted(): return lax.ppermute(array, axis, pairs)  5.98 us
    ppermute x1, starting transfers between devices, from_behind(): return lax.ppermute(block, axis, route)  0.52 us
  transfers between devices with their start and end apart: 5, of which 3 were waited for; matrix products, arithmetic and copies ran while one was open for 0% of the time, Pallas kernels for 27%

profile of v3, /device:TPU:0, one launch (start us, length us, event | category | flops | bytes accessed | tf_op | source)
XLA Modules:
  0.0 25.2 jit_solution(11265720942988666486)
XLA Ops:
  0.6 0.5 %collective-permute-start.1 = (bf16[1,256,1024]{2,1,0:T(8,128)(2,1)}, bf16[1,256,1024]{2,1,0:T(8,128)(2,1)S(1)}, u32[]{:S(2)}, u32[]{:S(2)}) collective-permute-start(bf16[1,256,1024]{2,1,0:T(8,128)(2,1)} %param.12), channel_id=1, source_target_pairs={{16,0},{0,16},{17,1},{1,17},{18,2},{2,18},{19,3},{3,19},{20,4},{4,... | collective-permute-start | bytes 1572872 | tf_op jit(solution)/shard_map/ppermute | solution.py:20
  1.2 0.0 copy-start
  1.2 0.0 copy-start.1
  1.2 0.0 copy-start.2
  1.2 1.0 %pack.1.block.own = bf16[272,256]{1,0:T(8,128)(2,1)S(1)} custom-call(bf16[1,256,128]{2,1,0:T(8,128)(2,1)} %keys.1, bf16[1,256,128]{2,1,0:T(8,128)(2,1)} %values.1, s32[1,256]{1,0:T(1,128)} %bitcast.1), custom_call_target="tpu_custom_call" | custom-call | flops 5368709120 | bytes 132096 | tf_op jit(solution)/shard_map/pack/pallas_call | solution.py:137
  2.2 4.4 %collective-permute-start = (bf16[272,256]{1,0:T(8,128)(2,1)S(1)}, bf16[272,256]{1,0:T(8,128)(2,1)S(1)}, u32[]{:S(2)}, u32[]{:S(2)}) collective-permute-start(bf16[272,256]{1,0:T(8,128)(2,1)S(1)} %pack.1.block.own), channel_id=1, source_target_pairs={{0,1},{1,2},{2,3},{3,4},{4,5},{5,6},{6,7},{7,8},{8,9},{9,10},{10,1... | collective-permute-start | bytes 417800 | tf_op jit(solution)/shard_map/ppermute | solution.py:26
  6.6 0.0 collective-permute-done.1.grads
  6.6 0.0 copy-done
  6.6 0.0 copy-done.1
  6.6 0.0 copy-done.2
  6.6 1.6 %own_block.1 = (bf16[256,2048]{1,0:T(8,128)(2,1)S(1)}, f32[256,256]{1,0:T(8,128)S(1)}, f32[8,256]{1,0:T(8,128)S(1)}, bf16[272,256]{1,0:T(8,128)(2,1)S(1)}) custom-call(bf16[1,256,1024]{2,1,0:T(8,128)(2,1)S(1)} %copy-done.1, bf16[1,256,1024]{2,1,0:T(8,128)(2,1)S(1)} %copy-done, bf16[1,256,1024]{2,1,0:T(8,128)(2,1)S(1)} %collective-permute-done.1.grads, ...), custom_call_target="tpu_custom_call" | custom-call | flops 536870912 | bytes 1720320 | tf_op jit(solution)/shard_map/own_block/pallas_call | solution.py:137
  8.3 3.4 %collective-permute-start.2 = (bf16[272,256]{1,0:T(8,128)(2,1)S(1)}, bf16[272,256]{1,0:T(8,128)(2,1)S(1)}, u32[]{:S(2)}, u32[]{:S(2)}) collective-permute-start(bf16[272,256]{1,0:T(8,128)(2,1)S(1)} %get-tuple-element.13), channel_id=1, source_target_pairs={{0,2},{1,3},{2,4},{3,5},{4,6},{5,7},{6,8},{7,9},{8,10},{9,11},{10,... | collective-permute-start | bytes 417800 | tf_op jit(solution)/shard_map/ppermute | solution.py:26
  11.7 0.0 collective-permute-done.block.near
  11.7 1.3 %near_block.1 = (bf16[256,2048]{1,0:T(8,128)(2,1)S(1)}, bf16[256,256]{1,0:T(8,128)(2,1)S(1)}) custom-call(bf16[1,256,1024]{2,1,0:T(8,128)(2,1)S(1)} %copy-done.1, bf16[1,256,1024]{2,1,0:T(8,128)(2,1)S(1)} %collective-permute-done.1.grads, f32[1,8,256]{2,1,0:T(8,128)S(1)} %copy-done.2, f32[8,256]{1,0:T(8,128)S(1)} %get-tuple-element.15.deltas, ...), custom_call_target="tpu_custom_call" | custom-call | flops 536870912 | bytes 1605632 | tf_op jit(solution)/shard_map/near_block/pallas_call | solution.py:137
  13.1 1.3 %collective-permute-start.3 = (bf16[256,256]{1,0:T(8,128)(2,1)S(1)}, bf16[256,256]{1,0:T(8,128)(2,1)S(1)}, u32[]{:S(2)}, u32[]{:S(2)}) collective-permute-start(bf16[256,256]{1,0:T(8,128)(2,1)S(1)} %get-tuple-element.18.before), channel_id=1, source_target_pairs={{1,0},{2,1},{3,2},{4,3},{5,4},{6,5},{7,6},{8,7},{9,8},{10,9},{11,1... | collective-permute-start | bytes 393224 | tf_op jit(solution)/shard_map/ppermute | solution.py:26
  14.4 0.6 %collective-permute-done.2.block.far = bf16[272,256]{1,0:T(8,128)(2,1)S(1)} collective-permute-done((bf16[272,256]{1,0:T(8,128)(2,1)S(1)}, bf16[272,256]{1,0:T(8,128)(2,1)S(1)}, u32[]{:S(2)}, u32[]{:S(2)}) %collective-permute-start.2) | collective-permute-done | bytes 139296 | tf_op jit(solution)/shard_map/ppermute | solution.py:26
  15.0 1.3 %far_block.1 = (bf16[256,2048]{1,0:T(8,128)(2,1)S(1)}, bf16[256,256]{1,0:T(8,128)(2,1)S(1)}) custom-call(bf16[1,256,1024]{2,1,0:T(8,128)(2,1)S(1)} %copy-done.1, bf16[1,256,1024]{2,1,0:T(8,128)(2,1)S(1)} %collective-permute-done.1.grads, f32[1,8,256]{2,1,0:T(8,128)S(1)} %copy-done.2, f32[8,256]{1,0:T(8,128)S(1)} %get-tuple-element.15.deltas, ...), custom_call_target="tpu_custom_call" | custom-call | flops 536870912 | bytes 1474560 | tf_op jit(solution)/shard_map/far_block/pallas_call | solution.py:137
  16.3 1.3 %collective-permute-start.4 = (bf16[256,256]{1,0:T(8,128)(2,1)S(1)}, bf16[256,256]{1,0:T(8,128)(2,1)S(1)}, u32[]{:S(2)}, u32[]{:S(2)}) collective-permute-start(bf16[256,256]{1,0:T(8,128)(2,1)S(1)} %get-tuple-element.20), channel_id=1, source_target_pairs={{2,0},{3,1},{4,2},{5,3},{6,4},{7,5},{8,6},{9,7},{10,8},{11,9},{12,... | collective-permute-start | bytes 393224 | tf_op jit(solution)/shard_map/ppermute | solution.py:26
  17.6 1.5 %query_grads.1 = bf16[1,256,1024]{2,1,0:T(8,128)(2,1)} custom-call(bf16[272,256]{1,0:T(8,128)(2,1)S(1)} %pack.1.block.own, bf16[272,256]{1,0:T(8,128)(2,1)S(1)} %collective-permute-done.block.near, bf16[272,256]{1,0:T(8,128)(2,1)S(1)} %collective-permute-done.2.block.far, bf16[256,2048]{1,0:T(8,128)(2,1)S(1)} %get-tuple-element.14.own_grads, ...), custom_call_target="tpu_custom_call" | custom-call | flops 402653184 | bytes 3563520 | tf_op jit(solution)/shard_map/query_grads/pallas_call | solution.py:137
  19.1 1.2 %collective-permute-done.3.near_sums = bf16[256,256]{1,0:T(8,128)(2,1)S(1)} collective-permute-done((bf16[256,256]{1,0:T(8,128)(2,1)S(1)}, bf16[256,256]{1,0:T(8,128)(2,1)S(1)}, u32[]{:S(2)}, u32[]{:S(2)}) %collective-permute-start.3) | collective-permute-done | bytes 131104 | tf_op jit(solution)/shard_map/ppermute | solution.py:26
  20.3 4.2 %collective-permute-done.4.far_sums = bf16[256,256]{1,0:T(8,128)(2,1)S(1)} collective-permute-done((bf16[256,256]{1,0:T(8,128)(2,1)S(1)}, bf16[256,256]{1,0:T(8,128)(2,1)S(1)}, u32[]{:S(2)}, u32[]{:S(2)}) %collective-permute-start.4) | collective-permute-done | bytes 131104 | tf_op jit(solution)/shard_map/ppermute | solution.py:26
  24.5 0.7 %add.1 = (bf16[1,256,128]{2,1,0:T(8,128)(2,1)}, bf16[1,256,128]{2,1,0:T(8,128)(2,1)}) custom-call(f32[256,256]{1,0:T(8,128)S(1)} %get-tuple-element.16.before.own_sums, bf16[256,256]{1,0:T(8,128)(2,1)S(1)} %collective-permute-done.3.near_sums, bf16[256,256]{1,0:T(8,128)(2,1)S(1)} %collective-permute-done.4.far_sums), custom_call_target="tpu_custom_call" | custom-call | bytes 524288 | tf_op jit(solution)/shard_map/add/pallas_call | solution.py:137
Async XLA Ops:
  0.6 6.0 %collective-permute-start.1 = (bf16[1,256,1024]{2,1,0:T(8,128)(2,1)}, bf16[1,256,1024]{2,1,0:T(8,128)(2,1)S(1)}, u32[]{:S(2)}, u32[]{:S(2)}) collective-permute-start(bf16[1,256,1024]{2,1,0:T(8,128)(2,1)} %param.12), channel_id=1, source_target_pairs={{16,0},{0,16},{17,1},{1,17},{18,2},{2,18},{19,3},{3,19},{20,4},{4,... | collective-permute-start | bytes 1572872 | tf_op jit(solution)/shard_map/ppermute | solution.py:20
  1.2 5.5 %copy-start = (bf16[1,256,1024]{2,1,0:T(8,128)(2,1)S(1)}, bf16[1,256,1024]{2,1,0:T(8,128)(2,1)}, u32[]{:S(2)}) copy-start(bf16[1,256,1024]{2,1,0:T(8,128)(2,1)} %attn_out.1) | copy-start | bytes 1572868
  1.2 5.5 %copy-start.1 = (bf16[1,256,1024]{2,1,0:T(8,128)(2,1)S(1)}, bf16[1,256,1024]{2,1,0:T(8,128)(2,1)}, u32[]{:S(2)}) copy-start(bf16[1,256,1024]{2,1,0:T(8,128)(2,1)} %queries.5) | copy-start | bytes 1572868
  1.2 5.5 %copy-start.2 = (f32[1,8,256]{2,1,0:T(8,128)S(1)}, f32[1,8,256]{2,1,0:T(8,128)}, u32[]{:S(2)}) copy-start(f32[1,8,256]{2,1,0:T(8,128)} %log_sums.5) | copy-start | bytes 24580
  2.2 9.6 %collective-permute-start = (bf16[272,256]{1,0:T(8,128)(2,1)S(1)}, bf16[272,256]{1,0:T(8,128)(2,1)S(1)}, u32[]{:S(2)}, u32[]{:S(2)}) collective-permute-start(bf16[272,256]{1,0:T(8,128)(2,1)S(1)} %pack.1.block.own), channel_id=1, source_target_pairs={{0,1},{1,2},{2,3},{3,4},{4,5},{5,6},{6,7},{7,8},{8,9},{9,10},{10,1... | collective-permute-start | bytes 417800 | tf_op jit(solution)/shard_map/ppermute | solution.py:26
  8.3 6.7 %collective-permute-start.2 = (bf16[272,256]{1,0:T(8,128)(2,1)S(1)}, bf16[272,256]{1,0:T(8,128)(2,1)S(1)}, u32[]{:S(2)}, u32[]{:S(2)}) collective-permute-start(bf16[272,256]{1,0:T(8,128)(2,1)S(1)} %get-tuple-element.13), channel_id=1, source_target_pairs={{0,2},{1,3},{2,4},{3,5},{4,6},{5,7},{6,8},{7,9},{8,10},{9,11},{10,... | collective-permute-start | bytes 417800 | tf_op jit(solution)/shard_map/ppermute | solution.py:26
  13.1 7.2 %collective-permute-start.3 = (bf16[256,256]{1,0:T(8,128)(2,1)S(1)}, bf16[256,256]{1,0:T(8,128)(2,1)S(1)}, u32[]{:S(2)}, u32[]{:S(2)}) collective-permute-start(bf16[256,256]{1,0:T(8,128)(2,1)S(1)} %get-tuple-element.18.before), channel_id=1, source_target_pairs={{1,0},{2,1},{3,2},{4,3},{5,4},{6,5},{7,6},{8,7},{9,8},{10,9},{11,1... | collective-permute-start | bytes 393224 | tf_op jit(solution)/shard_map/ppermute | solution.py:26
  16.3 8.2 %collective-permute-start.4 = (bf16[256,256]{1,0:T(8,128)(2,1)S(1)}, bf16[256,256]{1,0:T(8,128)(2,1)S(1)}, u32[]{:S(2)}, u32[]{:S(2)}) collective-permute-start(bf16[256,256]{1,0:T(8,128)(2,1)S(1)} %get-tuple-element.20), channel_id=1, source_target_pairs={{2,0},{3,1},{4,2},{5,3},{6,4},{7,5},{8,6},{9,7},{10,8},{11,9},{12,... | collective-permute-start | bytes 393224 | tf_op jit(solution)/shard_map/ppermute | solution.py:26

commit v4 on v3

--- a/solution.py
+++ b/solution.py
@@ -1,3 +1,5 @@
+import functools
+
 import jax
 import jax.numpy as jnp
 from jax import lax
@@ -7,6 +9,7 @@
 
 HOPS = 2
 DOC_ROWS = 16
+BACK_STRIDE = 4
 LOG2_E = 1.4426950408889634
 MASKED = -1e30
 
@@ -24,6 +27,40 @@
     devices = lax.axis_size(axis)
     pairs = [(i, i + by) for i in range(devices) if 0 <= i + by < devices]
     return lax.ppermute(array, axis, pairs)
+
+
+def full_routes(sections, shards, by, parity):
+    route = {}
+    for at in range(0, sections, 2):
+        there, back = at + parity, at + 1 - parity
+        for c in range(shards - by):
+            route[there, c] = (there, c + by)
+        free = set(range(shards))
+        for last in range(shards - by, shards):
+            first = last - shards + by
+            way = [(there, last)] + [(back, c) for c in range(last, by - 1, -BACK_STRIDE)] + [(back, first), (there, first)]
+            free -= {c for section, c in way if section == back}
+            route.update(zip(way, way[1:]))
+        for lane in range(BACK_STRIDE):
+            rest = [c for c in sorted(free) if c % BACK_STRIDE == lane]
+            pairs = [(c, c + 1) for c in rest if c + 1 in free] if by > 1 else []
+            if by == 1:
+                pairs = list(zip(rest[0::2], rest[1::2])) if len(rest) % 2 == 0 else []
+                if not pairs:
+                    route.update({(back, c): (back, rest[k - len(rest) + 1]) for k, c in enumerate(rest)})
+            for c, d in pairs:
+                route.update({(back, c): (back, d), (back, d): (back, c)})
+    full = sections * shards
+    whole = len(route) == full and len(set(route.values())) == full and all(a != b for a, b in route.items())
+    return [(a * shards + c, b * shards + d) for (a, c), (b, d) in sorted(route.items())] if whole else None
+
+
+def behind(block, by):
+    sections, shards = lax.axis_size("section"), lax.axis_size("ctx")
+    routes = [full_routes(sections, shards, by, parity) for parity in (0, 1)] if sections % 2 == 0 and shards >= 4 * BACK_STRIDE else [None]
+    if None in routes:
+        return [shifted(block, "ctx", by)]
+    return [lax.ppermute(block, ("section", "ctx"), route) for route in routes]
 
 
 def dot_nt(a, b):
@@ -102,11 +139,21 @@
     block_grads(queries, grads, log_sums, delta_of, block, bias, score_grads, weights_low, sums)
 
 
-def hop_kernel(queries, grads, log_sums, deltas, own, block, before, score_grads, sums, bias, weights_low):
+def hop_kernel(hop, queries, grads, log_sums, deltas, own, before, *refs):
+    candidates, (score_grads, sums, block, bias, weights_low) = refs[:-5], refs[-5:]
     rows = queries.shape[1]
-    width = block.shape[1] // 2
+    width = own.shape[1] // 2
+    if len(candidates) == 1:
+        block[...] = candidates[0][...]
+    for parity, candidate in enumerate(candidates[: len(candidates) // 2 * 2]):
+
+        @pl.when(lax.axis_index("section") % 2 == parity)
+        def _():
+            block[...] = candidate[...]
+
     docs = own[rows : rows + DOC_ROWS, :].astype(F32)[0:1]
     far_docs = block[rows : rows + DOC_ROWS, :].astype(F32)[0:1]
+    far_docs = jnp.where(lax.axis_index("ctx") >= hop, far_docs, 0.0)
     bias[...] = jnp.where(column_of(far_docs, width) == docs, 0.0, MASKED)
     delta_of = lambda head, part, g: deltas[head : head + 1, :]
     block_grads(queries, grads, log_sums, delta_of, block, bias, score_grads, weights_low, sums)
@@ -165,7 +212,7 @@
         [pltpu.VMEM((1, rows), jnp.int32), pltpu.SemaphoreType.DMA((3,))],
         3,
     )
-    near = shifted(own, "ctx", 1)
+    near = behind(own, 1)
     own_grads, own_sums, deltas, own_again = call(
         own_kernel,
         "own_block",
@@ -174,11 +221,16 @@
         4 * flops,
         scratch,
     )
-    far = shifted(own_again, "ctx", 2)
-    hop = lambda name, block, before: call(hop_kernel, name, (score_grads, sums(BF16)), (queries, grads, log_sums, deltas, own, block, before), 4 * flops, scratch)
-    near_grads, near_sums = hop("near_block", near, own_sums)
+    far = behind(own_again, 2)
+    def block_of(name, hop, before, candidates):
+        outs = (score_grads, sums(BF16), shape(own.shape, BF16))
+        return call(
+            functools.partial(hop_kernel, hop), name, outs, (queries, grads, log_sums, deltas, own, before, *candidates), 4 * flops, scratch
+        )
+
+    near_grads, near_sums, near = block_of("near_block", 1, own_sums, near)
     near_back = shifted(near_sums, "ctx", -1)
-    far_grads, far_sums = hop("far_block", far, near_sums)
+    far_grads, far_sums, far = block_of("far_block", 2, near_sums, far)
     far_back = shifted(far_sums, "ctx", -2)
     (grad_queries,) = call(query_kernel, "query_grads", (shape(queries.shape, BF16),), (own, near, far, own_grads, near_grads, far_grads), 3 * flops)
     grad_keys, grad_values = call(add_kernel, "add", (shape(keys.shape, BF16), shape(values.shape, BF16)), (own_sums, near_back, far_back))

time: 25.4 us -> 23.7 us (0.933)
  starting transfers between devices: 11 us -> 8.83 us
  waiting for transfers between devices: 5.98 us -> 6.44 us
    ppermute x4 -> x2, starting transfers between devices: 10.4 us -> 2.58 us  [shifted(): return lax.ppermute(array, axis, pairs)]
    ppermute x0 -> x4, starting transfers between devices: none -> 5.72 us  [behind(): return [lax.ppermute(block, ('section', 'ctx'), route) for route in routes]]
    ppermute x0 -> x4, waiting for transfers between devices: none -> 2.38 us  [behind(): return [lax.ppermute(block, ('section', 'ctx'), route) for route in routes]]
    ppermute x4 -> x2, waiting for transfers between devices: 5.98 us -> 4.06 us  [shifted(): return lax.ppermute(array, axis, pairs)]
  transfers between devices with their start and end apart: 5 -> 7, of which waited for: 3 -> 4; matrix products, arithmetic and copies ran while one was open for 0% -> 0% of each run, Pallas kernels for 27% -> 29%
where the time goes in v4:
time: 23.7 us; the launch traced here: 23.5 us
  starting transfers between devices  8.83 us (37%)
  Pallas kernels  7.55 us (32%)
  waiting for transfers between devices  6.44 us (27%)
  between operations  0.71 us (3%)
    pallas_call x6, Pallas kernels, call(): pl.pallas_call(kernel, out_shape=outs, in_specs=[pl.BlockSpec(memory_spac...  7.55 us
    ppermute x4, starting transfers between devices, behind(): return [lax.ppermute(block, ('section', 'ctx'), route) for route in routes]  5.72 us
    ppermute x2, waiting for transfers between devices, shifted(): return lax.ppermute(array, axis, pairs)  4.06 us
    ppermute x2, starting transfers between devices, shifted(): return lax.ppermute(array, axis, pairs)  2.58 us
    ppermute x4, waiting for transfers between devices, behind(): return [lax.ppermute(block, ('section', 'ctx'), route) for route in routes]  2.38 us
    ppermute x1, starting transfers between devices, from_behind(): return lax.ppermute(block, axis, route)  0.52 us
  transfers between devices with their start and end apart: 7, of which 4 were waited for; matrix products, arithmetic and copies ran while one was open for 0% of the time, Pallas kernels for 29%

profile of v4, /device:TPU:0, one launch (start us, length us, event | category | flops | bytes accessed | tf_op | source)
XLA Modules:
  0.0 23.5 jit_solution(10778963381538946942)
XLA Ops:
  0.6 0.5 %collective-permute-start = (bf16[1,256,1024]{2,1,0:T(8,128)(2,1)}, bf16[1,256,1024]{2,1,0:T(8,128)(2,1)S(1)}, u32[]{:S(2)}, u32[]{:S(2)}) collective-permute-start(bf16[1,256,1024]{2,1,0:T(8,128)(2,1)} %param.12), channel_id=1, source_target_pairs={{16,0},{0,16},{17,1},{1,17},{18,2},{2,18},{19,3},{3,19},{20,4},{4,... | collective-permute-start | bytes 1572872 | tf_op jit(solution)/shard_map/ppermute | solution.py:23
  1.2 0.0 copy-start
  1.2 0.0 copy-start.1
  1.2 0.0 copy-start.2
  1.2 1.0 %pack.1.block.own = bf16[272,256]{1,0:T(8,128)(2,1)S(1)} custom-call(bf16[1,256,128]{2,1,0:T(8,128)(2,1)} %keys.1, bf16[1,256,128]{2,1,0:T(8,128)(2,1)} %values.1, s32[1,256]{1,0:T(1,128)} %bitcast.1), custom_call_target="tpu_custom_call" | custom-call | flops 5368709120 | bytes 132096 | tf_op jit(solution)/shard_map/pack/pallas_call | solution.py:184
  2.2 2.6 %collective-permute-start.1 = (bf16[272,256]{1,0:T(8,128)(2,1)S(1)}, bf16[272,256]{1,0:T(8,128)(2,1)S(1)}, u32[]{:S(2)}, u32[]{:S(2)}) collective-permute-start(bf16[272,256]{1,0:T(8,128)(2,1)S(1)} %pack.1.block.own), channel_id=1, source_target_pairs={{0,1},{1,2},{2,3},{3,4},{4,5},{5,6},{6,7},{7,8},{8,9},{9,10},{10,1... | collective-permute-start | bytes 417800 | tf_op jit(solution)/shard_map/ppermute | solution.py:63
  4.7 0.0 collective-permute-start.2
  4.7 0.0 collective-permute-done.grads
  4.7 0.0 copy-done
  4.8 0.0 copy-done.1
  4.8 0.0 copy-done.2
  4.8 1.6 %own_block.1 = (bf16[256,2048]{1,0:T(8,128)(2,1)S(1)}, f32[256,256]{1,0:T(8,128)S(1)}, f32[8,256]{1,0:T(8,128)S(1)}, bf16[272,256]{1,0:T(8,128)(2,1)S(1)}) custom-call(bf16[1,256,1024]{2,1,0:T(8,128)(2,1)S(1)} %copy-done.1, bf16[1,256,1024]{2,1,0:T(8,128)(2,1)S(1)} %copy-done, bf16[1,256,1024]{2,1,0:T(8,128)(2,1)S(1)} %collective-permute-done.grads, ...), custom_call_target="tpu_custom_call" | custom-call | flops 536870912 | bytes 1720320 | tf_op jit(solution)/shard_map/own_block/pallas_call | solution.py:184
  6.4 3.1 %collective-permute-start.3 = (bf16[272,256]{1,0:T(8,128)(2,1)S(1)}, bf16[272,256]{1,0:T(8,128)(2,1)S(1)}, u32[]{:S(2)}, u32[]{:S(2)}) collective-permute-start(bf16[272,256]{1,0:T(8,128)(2,1)S(1)} %get-tuple-element.19), channel_id=1, source_target_pairs={{0,2},{1,3},{2,4},{3,5},{4,6},{5,7},{6,8},{7,9},{8,10},{9,11},{10,... | collective-permute-start | bytes 417800 | tf_op jit(solution)/shard_map/ppermute | solution.py:63
  9.6 0.0 collective-permute-start.4
  9.6 0.0 collective-permute-done.1.refs_0_
  9.6 1.1 %collective-permute-done.2.refs_1_ = bf16[272,256]{1,0:T(8,128)(2,1)S(1)} collective-permute-done((bf16[272,256]{1,0:T(8,128)(2,1)S(1)}, bf16[272,256]{1,0:T(8,128)(2,1)S(1)}, u32[]{:S(2)}, u32[]{:S(2)}) %collective-permute-start.2) | collective-permute-done | bytes 139296 | tf_op jit(solution)/shard_map/ppermute | solution.py:63
  10.7 1.4 %near_block.1 = (bf16[256,2048]{1,0:T(8,128)(2,1)S(1)}, bf16[256,256]{1,0:T(8,128)(2,1)S(1)}, bf16[272,256]{1,0:T(8,128)(2,1)S(1)}) custom-call(bf16[1,256,1024]{2,1,0:T(8,128)(2,1)S(1)} %copy-done.1, bf16[1,256,1024]{2,1,0:T(8,128)(2,1)S(1)} %collective-permute-done.grads, f32[1,8,256]{2,1,0:T(8,128)S(1)} %copy-done.2, ...), custom_call_target="tpu_custom_call" | custom-call | flops 536870912 | bytes 1744896 | tf_op jit(solution)/shard_map/near_block/pallas_call | solution.py:184
  12.1 1.3 %collective-permute-start.5 = (bf16[256,256]{1,0:T(8,128)(2,1)S(1)}, bf16[256,256]{1,0:T(8,128)(2,1)S(1)}, u32[]{:S(2)}, u32[]{:S(2)}) collective-permute-start(bf16[256,256]{1,0:T(8,128)(2,1)S(1)} %get-tuple-element.18.before), channel_id=1, source_target_pairs={{1,0},{2,1},{3,2},{4,3},{5,4},{6,5},{7,6},{8,7},{9,8},{10,9},{11,1... | collective-permute-start | bytes 393224 | tf_op jit(solution)/shard_map/ppermute | solution.py:29
  13.4 0.0 collective-permute-done.3.refs_0_
  13.4 1.2 %collective-permute-done.4.refs_1_ = bf16[272,256]{1,0:T(8,128)(2,1)S(1)} collective-permute-done((bf16[272,256]{1,0:T(8,128)(2,1)S(1)}, bf16[272,256]{1,0:T(8,128)(2,1)S(1)}, u32[]{:S(2)}, u32[]{:S(2)}) %collective-permute-start.4) | collective-permute-done | bytes 139296 | tf_op jit(solution)/shard_map/ppermute | solution.py:63
  14.6 1.4 %far_block.1 = (bf16[256,2048]{1,0:T(8,128)(2,1)S(1)}, bf16[256,256]{1,0:T(8,128)(2,1)S(1)}, bf16[272,256]{1,0:T(8,128)(2,1)S(1)}) custom-call(bf16[1,256,1024]{2,1,0:T(8,128)(2,1)S(1)} %copy-done.1, bf16[1,256,1024]{2,1,0:T(8,128)(2,1)S(1)} %collective-permute-done.grads, f32[1,8,256]{2,1,0:T(8,128)S(1)} %copy-done.2, ...), custom_call_target="tpu_custom_call" | custom-call | flops 536870912 | bytes 1613824 | tf_op jit(solution)/shard_map/far_block/pallas_call | solution.py:184
  16.0 1.3 %collective-permute-start.6 = (bf16[256,256]{1,0:T(8,128)(2,1)S(1)}, bf16[256,256]{1,0:T(8,128)(2,1)S(1)}, u32[]{:S(2)}, u32[]{:S(2)}) collective-permute-start(bf16[256,256]{1,0:T(8,128)(2,1)S(1)} %get-tuple-element.24), channel_id=1, source_target_pairs={{2,0},{3,1},{4,2},{5,3},{6,4},{7,5},{8,6},{9,7},{10,8},{11,9},{12,... | collective-permute-start | bytes 393224 | tf_op jit(solution)/shard_map/ppermute | solution.py:29
  17.3 1.5 %query_grads.1 = bf16[1,256,1024]{2,1,0:T(8,128)(2,1)} custom-call(bf16[272,256]{1,0:T(8,128)(2,1)S(1)} %pack.1.block.own, bf16[272,256]{1,0:T(8,128)(2,1)S(1)} %get-tuple-element.17.near, bf16[272,256]{1,0:T(8,128)(2,1)S(1)} %get-tuple-element.20.far, bf16[256,2048]{1,0:T(8,128)(2,1)S(1)} %get-tuple-element.21.own_grads, ...), custom_call_target="tpu_custom_call" | custom-call | flops 402653184 | bytes 3563520 | tf_op jit(solution)/shard_map/query_grads/pallas_call | solution.py:184
  18.8 0.1 collective-permute-done.5.near_sums
  18.9 3.9 %collective-permute-done.6.far_sums = bf16[256,256]{1,0:T(8,128)(2,1)S(1)} collective-permute-done((bf16[256,256]{1,0:T(8,128)(2,1)S(1)}, bf16[256,256]{1,0:T(8,128)(2,1)S(1)}, u32[]{:S(2)}, u32[]{:S(2)}) %collective-permute-start.6) | collective-permute-done | bytes 131104 | tf_op jit(solution)/shard_map/ppermute | solution.py:29
  22.8 0.7 %add.1 = (bf16[1,256,128]{2,1,0:T(8,128)(2,1)}, bf16[1,256,128]{2,1,0:T(8,128)(2,1)}) custom-call(f32[256,256]{1,0:T(8,128)S(1)} %get-tuple-element.16.before.own_sums, bf16[256,256]{1,0:T(8,128)(2,1)S(1)} %collective-permute-done.5.near_sums, bf16[256,256]{1,0:T(8,128)(2,1)S(1)} %collective-permute-done.6.far_sums), custom_call_target="tpu_custom_call" | custom-call | bytes 524288 | tf_op jit(solution)/shard_map/add/pallas_call | solution.py:184
Async XLA Ops:
  0.6 4.1 %collective-permute-start = (bf16[1,256,1024]{2,1,0:T(8,128)(2,1)}, bf16[1,256,1024]{2,1,0:T(8,128)(2,1)S(1)}, u32[]{:S(2)}, u32[]{:S(2)}) collective-permute-start(bf16[1,256,1024]{2,1,0:T(8,128)(2,1)} %param.12), channel_id=1, source_target_pairs={{16,0},{0,16},{17,1},{1,17},{18,2},{2,18},{19,3},{3,19},{20,4},{4,... | collective-permute-start | bytes 1572872 | tf_op jit(solution)/shard_map/ppermute | solution.py:23
  1.2 3.6 %copy-start = (bf16[1,256,1024]{2,1,0:T(8,128)(2,1)S(1)}, bf16[1,256,1024]{2,1,0:T(8,128)(2,1)}, u32[]{:S(2)}) copy-start(bf16[1,256,1024]{2,1,0:T(8,128)(2,1)} %attn_out.1) | copy-start | bytes 1572868
  1.2 3.6 %copy-start.1 = (bf16[1,256,1024]{2,1,0:T(8,128)(2,1)S(1)}, bf16[1,256,1024]{2,1,0:T(8,128)(2,1)}, u32[]{:S(2)}) copy-start(bf16[1,256,1024]{2,1,0:T(8,128)(2,1)} %queries.5) | copy-start | bytes 1572868
  1.2 3.6 %copy-start.2 = (f32[1,8,256]{2,1,0:T(8,128)S(1)}, f32[1,8,256]{2,1,0:T(8,128)}, u32[]{:S(2)}) copy-start(f32[1,8,256]{2,1,0:T(8,128)} %log_sums.5) | copy-start | bytes 24580
  2.2 7.4 %collective-permute-start.1 = (bf16[272,256]{1,0:T(8,128)(2,1)S(1)}, bf16[272,256]{1,0:T(8,128)(2,1)S(1)}, u32[]{:S(2)}, u32[]{:S(2)}) collective-permute-start(bf16[272,256]{1,0:T(8,128)(2,1)S(1)} %pack.1.block.own), channel_id=1, source_target_pairs={{0,1},{1,2},{2,3},{3,4},{4,5},{5,6},{6,7},{7,8},{8,9},{9,10},{10,1... | collective-permute-start | bytes 417800 | tf_op jit(solution)/shard_map/ppermute | solution.py:63
  4.7 6.0 %collective-permute-start.2 = (bf16[272,256]{1,0:T(8,128)(2,1)S(1)}, bf16[272,256]{1,0:T(8,128)(2,1)S(1)}, u32[]{:S(2)}, u32[]{:S(2)}) collective-permute-start(bf16[272,256]{1,0:T(8,128)(2,1)S(1)} %pack.1.block.own), channel_id=1, source_target_pairs={{0,16},{1,5},{2,6},{3,0},{4,8},{5,1},{6,2},{7,3},{8,12},{9,13},{10... | collective-permute-start | bytes 417800 | tf_op jit(solution)/shard_map/ppermute | solution.py:63
  6.4 7.0 %collective-permute-start.3 = (bf16[272,256]{1,0:T(8,128)(2,1)S(1)}, bf16[272,256]{1,0:T(8,128)(2,1)S(1)}, u32[]{:S(2)}, u32[]{:S(2)}) collective-permute-start(bf16[272,256]{1,0:T(8,128)(2,1)S(1)} %get-tuple-element.19), channel_id=1, source_target_pairs={{0,2},{1,3},{2,4},{3,5},{4,6},{5,7},{6,8},{7,9},{8,10},{9,11},{10,... | collective-permute-start | bytes 417800 | tf_op jit(solution)/shard_map/ppermute | solution.py:63
  9.6 5.1 %collective-permute-start.4 = (bf16[272,256]{1,0:T(8,128)(2,1)S(1)}, bf16[272,256]{1,0:T(8,128)(2,1)S(1)}, u32[]{:S(2)}, u32[]{:S(2)}) collective-permute-start(bf16[272,256]{1,0:T(8,128)(2,1)S(1)} %get-tuple-element.19), channel_id=1, source_target_pairs={{0,16},{1,17},{2,0},{3,1},{4,5},{5,4},{6,2},{7,3},{8,9},{9,8},{10,... | collective-permute-start | bytes 417800 | tf_op jit(solution)/shard_map/ppermute | solution.py:63
  12.1 6.9 %collective-permute-start.5 = (bf16[256,256]{1,0:T(8,128)(2,1)S(1)}, bf16[256,256]{1,0:T(8,128)(2,1)S(1)}, u32[]{:S(2)}, u32[]{:S(2)}) collective-permute-start(bf16[256,256]{1,0:T(8,128)(2,1)S(1)} %get-tuple-element.18.before), channel_id=1, source_target_pairs={{1,0},{2,1},{3,2},{4,3},{5,4},{6,5},{7,6},{8,7},{9,8},{10,9},{11,1... | collective-permute-start | bytes 393224 | tf_op jit(solution)/shard_map/ppermute | solution.py:29
  16.0 6.9 %collective-permute-start.6 = (bf16[256,256]{1,0:T(8,128)(2,1)S(1)}, bf16[256,256]{1,0:T(8,128)(2,1)S(1)}, u32[]{:S(2)}, u32[]{:S(2)}) collective-permute-start(bf16[256,256]{1,0:T(8,128)(2,1)S(1)} %get-tuple-element.24), channel_id=1, source_target_pairs={{2,0},{3,1},{4,2},{5,3},{6,4},{7,5},{8,6},{9,7},{10,8},{11,9},{12,... | collective-permute-start | bytes 393224 | tf_op jit(solution)/shard_map/ppermute | solution.py:29

commit v5 on v4

--- a/solution.py
+++ b/solution.py
@@ -9,6 +9,10 @@
 
 HOPS = 2
 DOC_ROWS = 16
+LAST_ROW = 8
+COUNT_ROW = 9
+FACT_ROWS = 8
+NONE, FEW_KEYS, FEW_QUERIES, ALL = range(4)
 BACK_STRIDE = 4
 LOG2_E = 1.4426950408889634
 MASKED = -1e30
@@ -71,10 +75,6 @@
     return lax.dot_general(a, b, (((1,), (0,)), ((), ())), preferred_element_type=F32)
 
 
-def vmem(count):
-    return [pl.BlockSpec(memory_space=pltpu.VMEM)] * count
-
-
 def pack_kernel(keys, values, docs, packed, docs_here, sems):
     rows, width = keys.shape[1:]
     copies = [
@@ -85,8 +85,12 @@
     for copy in copies:
         copy.start()
     copies[0].wait()
-    docs_row = (docs_here[...] + 1).astype(F32).astype(BF16)
-    packed[rows : rows + DOC_ROWS, :] = jnp.broadcast_to(docs_row, (DOC_ROWS, docs_row.shape[1]))
+    docs_row = docs_here[...]
+    last = jnp.max(docs_row, axis=1, keepdims=True)
+    last_count = jnp.sum((docs_row == last).astype(F32), axis=1, keepdims=True)
+    row_at = lax.broadcasted_iota(jnp.int32, (DOC_ROWS, rows), 0)
+    table = jnp.where(row_at == LAST_ROW, last.astype(F32) + 1, jnp.where(row_at == COUNT_ROW, last_count, docs_row.astype(F32) + 1))
+    packed[rows : rows + DOC_ROWS, :] = table.astype(BF16)
     for copy in copies[1:]:
         copy.wait()
 
@@ -97,25 +101,36 @@
     return jnp.concatenate([column] * (rows // width), axis=1)
 
 
-def block_grads(queries, grads, log_sums, delta_of, block, bias, score_grads, weights_low, sums):
+def block_grads(queries, grads, log_sums, delta_of, block, bias, score_grads, weights_low, sums, first_key, query_rows):
     rows = queries.shape[1]
     heads = log_sums.shape[1]
     width = queries.shape[2] // heads
     scale = float(width) ** -0.5
-    parts = [slice(head * width, (head + 1) * width) for head in range(heads)]
-    for head, part in enumerate(parts):
-        columns = slice(head * rows, (head + 1) * rows)
-        g = grads[0, :, part]
-        delta = delta_of(head, part, g)
-        lse = log_sums[0, head : head + 1, :] * LOG2_E
-        scores = dot_nt(block[0:rows, 0:width], queries[0, :, part])
-        weights = jnp.exp2(scores * (scale * LOG2_E) - lse + bias[...])
-        weight_grads = dot_nt(block[0:rows, width : 2 * width], g)
-        score_grads[:, columns] = (weights * (weight_grads - delta)).astype(BF16)
-        weights_low[:, columns] = weights.astype(BF16)
-    stacked = lambda ref: jnp.concatenate([ref[0, :, part] for part in parts], axis=0)
-    sums[:, 0:width] = (dot_nn(score_grads[...], stacked(queries)) * scale).astype(sums.dtype)
-    sums[:, width : 2 * width] = dot_nn(weights_low[...], stacked(grads)).astype(sums.dtype)
+    beside = rows // query_rows
+    key_rows = slice(first_key, rows)
+    side = lambda pieces: pieces[0] if len(pieces) == 1 else jnp.concatenate(pieces, axis=1)
+    under = lambda pieces: pieces[0] if len(pieces) == 1 else jnp.concatenate(pieces, axis=0)
+    part = lambda ref, head: ref[0, 0:query_rows, head * width : (head + 1) * width]
+    columns = lambda head: slice(head * rows, head * rows + query_rows)
+    masked = side([bias[key_rows, 0:query_rows]] * beside)
+    for head in range(0, heads, beside):
+        group = range(head, head + beside)
+        g = under([part(grads, h) for h in group])
+        delta = side([delta_of(h, part(grads, h))[:, 0:query_rows] for h in group])
+        lse = side([log_sums[0, h : h + 1, 0:query_rows] for h in group]) * LOG2_E
+        scores = dot_nt(block[key_rows, 0:width], under([part(queries, h) for h in group]))
+        weights = jnp.exp2(scores * (scale * LOG2_E) - lse + masked)
+        weight_grads = dot_nt(block[key_rows, width : 2 * width], g)
+        low = (weights * (weight_grads - delta)).astype(BF16)
+        weights = weights.astype(BF16)
+        for at, h in enumerate(group):
+            here = slice(at * query_rows, (at + 1) * query_rows)
+            score_grads[key_rows, columns(h)] = low[:, here]
+            weights_low[key_rows, columns(h)] = weights[:, here]
+    everything = lambda ref: ref[key_rows, :] if beside == 1 else side([ref[key_rows, columns(h)] for h in range(heads)])
+    stacked = lambda ref: under([part(ref, h) for h in range(heads)])
+    sums[key_rows, 0:width] = (dot_nn(everything(score_grads), stacked(queries)) * scale).astype(sums.dtype)
+    sums[key_rows, width : 2 * width] = dot_nn(everything(weights_low), stacked(grads)).astype(sums.dtype)
 
 
 def own_kernel(queries, attn_out, grads, log_sums, block, score_grads, sums, deltas, block_again, bias, weights_low):
@@ -126,23 +141,25 @@
     key_at = lax.broadcasted_iota(jnp.int32, (rows, rows), 0)
     query_at = lax.broadcasted_iota(jnp.int32, (rows, rows), 1)
     bias[...] = jnp.where((column_of(docs, width) == docs) & (key_at <= query_at), 0.0, MASKED)
+    first_count = jnp.sum((docs == docs[:, 0:1]).astype(F32), axis=1, keepdims=True)
+    deltas[log_sums.shape[1] :, :] = jnp.broadcast_to(first_count, (FACT_ROWS, rows))
     one = jnp.ones((8, width), BF16)
 
-    def delta_of(head, part, g):
-        product = g.astype(F32) * attn_out[0, :, part].astype(F32)
+    def delta_of(head, g):
+        product = g.astype(F32) * attn_out[0, :, head * width : (head + 1) * width].astype(F32)
         high = product.astype(BF16)
         low = (product - high.astype(F32)).astype(BF16)
         delta = (dot_nt(one, high) + dot_nt(one, low))[0:1]
         deltas[head : head + 1, :] = delta
         return delta
 
-    block_grads(queries, grads, log_sums, delta_of, block, bias, score_grads, weights_low, sums)
+    block_grads(queries, grads, log_sums, delta_of, block, bias, score_grads, weights_low, sums, 0, rows)
 
 
 def hop_kernel(hop, queries, grads, log_sums, deltas, own, before, *refs):
     candidates, (score_grads, sums, block, bias, weights_low) = refs[:-5], refs[-5:]
     rows = queries.shape[1]
-    width = own.shape[1] // 2
+    half = rows // 2
     if len(candidates) == 1:
         block[...] = candidates[0][...]
     for parity, candidate in enumerate(candidates[: len(candidates) // 2 * 2]):
@@ -152,11 +169,39 @@
             block[...] = candidate[...]
 
     docs = own[rows : rows + DOC_ROWS, :].astype(F32)[0:1]
-    far_docs = block[rows : rows + DOC_ROWS, :].astype(F32)[0:1]
-    far_docs = jnp.where(lax.axis_index("ctx") >= hop, far_docs, 0.0)
-    bias[...] = jnp.where(column_of(far_docs, width) == docs, 0.0, MASKED)
-    delta_of = lambda head, part, g: deltas[head : head + 1, :]
-    block_grads(queries, grads, log_sums, delta_of, block, bias, score_grads, weights_low, sums)
+    table = block[rows : rows + DOC_ROWS, :].astype(F32)
+    same = (table[LAST_ROW : LAST_ROW + 1] == docs[:, 0:1]) & (lax.axis_index("ctx") >= hop)
+    key_count = jnp.where(same, table[COUNT_ROW : COUNT_ROW + 1], 0.0)
+    query_count = deltas[log_sums.shape[1] : log_sums.shape[1] + 1, :]
+    key_at = lax.broadcasted_iota(jnp.int32, (rows, rows), 0).astype(F32)
+    bias[...] = jnp.where((key_at >= rows - key_count) & (docs == docs[:, 0:1]), 0.0, MASKED)
+    some = jnp.where(query_count <= half, FEW_QUERIES, ALL)
+    mode = jnp.where(key_count == 0, NONE, jnp.where(key_count <= half, FEW_KEYS, some))[0, 0]
+    delta_of = lambda head, g: deltas[head : head + 1, :]
+    work = functools.partial(block_grads, queries, grads, log_sums, delta_of, block, bias, score_grads, weights_low, sums)
+
+    @pl.when(mode == NONE)
+    def _():
+        score_grads[...] = jnp.zeros_like(score_grads)
+        sums[...] = jnp.zeros_like(sums)
+
+    @pl.when(mode == FEW_KEYS)
+    def _():
+        score_grads[0:half, :] = jnp.zeros((half, score_grads.shape[1]), BF16)
+        sums[0:half, :] = jnp.zeros((half, sums.shape[1]), BF16)
+        work(half, rows)
+
+    @pl.when(mode == FEW_QUERIES)
+    def _():
+        for head in range(score_grads.shape[1] // rows):
+            score_grads[:, head * rows + half : (head + 1) * rows] = jnp.zeros((rows, rows - half), BF16)
+        work(0, half)
+
+    if hop < HOPS:
+
+        @pl.when(mode == ALL)
+        def _():
+            work(0, rows)
 
 
 def query_kernel(own, near, far, own_grads, near_grads, far_grads, grad_queries):
@@ -181,6 +226,7 @@
 def call(kernel, name, outs, args, flops=0, scratch=(), from_hbm=0, limit=8):
     args = [pltpu.with_memory_space_constraint(a, pltpu.HBM) for a in args[:from_hbm]] + list(args[from_hbm:])
     moved = sum(a.size * a.dtype.itemsize for a in args)
+    vmem = lambda count: [pl.BlockSpec(memory_space=pltpu.VMEM)] * count
     return pl.pallas_call(
         kernel,
         out_shape=outs,
@@ -216,7 +262,7 @@
     own_grads, own_sums, deltas, own_again = call(
         own_kernel,
         "own_block",
-        (score_grads, sums(F32), shape((heads, rows), F32), shape(own.shape, BF16)),
+        (score_grads, sums(F32), shape((heads + FACT_ROWS, rows), F32), shape(own.shape, BF16)),
         (queries, attn_out, grads, log_sums, own),
         4 * flops,
         scratch,

time: 23.7 us -> 22.8 us (0.962)
  Pallas kernels: 7.55 us -> 5.3 us
  waiting for transfers between devices: 6.44 us -> 7.67 us
    pallas_call x6, Pallas kernels: 7.55 us -> 5.3 us  [call(): pl.pallas_call(kernel, out_shape=outs, in_specs=[pl.BlockSpec(memory_spac...]
    ppermute x4, waiting for transfers between devices: 2.38 us -> 3.52 us  [behind(): return [lax.ppermute(block, ('section', 'ctx'), route) for route in routes]]
  transfers between devices with their start and end apart: 7 -> 7, of which waited for: 4 -> 5; matrix products, arithmetic and copies ran while one was open for 0% -> 0% of each run, Pallas kernels for 29% -> 21%
where the time goes in v5:
time: 22.8 us; the launch traced here: 22.5 us
  starting transfers between devices  8.82 us (39%)
  waiting for transfers between devices  7.67 us (34%)
  Pallas kernels  5.3 us (23%)
  between operations  0.7 us (3%)
    ppermute x4, starting transfers between devices, behind(): return [lax.ppermute(block, ('section', 'ctx'), route) for route in routes]  5.72 us
    pallas_call x6, Pallas kernels, call(): pl.pallas_call(kernel, out_shape=outs, in_specs=[pl.BlockSpec(memory_spac...  5.3 us
    ppermute x2, waiting for transfers between devices, shifted(): return lax.ppermute(array, axis, pairs)  4.15 us
    ppermute x4, waiting for transfers between devices, behind(): return [lax.ppermute(block, ('section', 'ctx'), route) for route in routes]  3.52 us
    ppermute x2, starting transfers between devices, shifted(): return lax.ppermute(array, axis, pairs)  2.58 us
    ppermute x1, starting transfers between devices, from_behind(): return lax.ppermute(block, axis, route)  0.52 us
  transfers between devices with their start and end apart: 7, of which 5 were waited for; matrix products, arithmetic and copies ran while one was open for 0% of the time, Pallas kernels for 21%

profile of v5, /device:TPU:0, one launch (start us, length us, event | category | flops | bytes accessed | tf_op | source)
XLA Modules:
  0.0 22.5 jit_solution(17372652623761635214)
XLA Ops:
  0.6 0.5 %collective-permute-start = (bf16[1,256,1024]{2,1,0:T(8,128)(2,1)}, bf16[1,256,1024]{2,1,0:T(8,128)(2,1)S(1)}, u32[]{:S(2)}, u32[]{:S(2)}) collective-permute-start(bf16[1,256,1024]{2,1,0:T(8,128)(2,1)} %param.12), channel_id=1, source_target_pairs={{16,0},{0,16},{17,1},{1,17},{18,2},{2,18},{19,3},{3,19},{20,4},{4,... | collective-permute-start | bytes 1572872 | tf_op jit(solution)/shard_map/ppermute | solution.py:27
  1.2 0.0 copy-start
  1.2 0.0 copy-start.1
  1.2 0.0 copy-start.2
  1.2 1.0 %pack.1.block.own = bf16[272,256]{1,0:T(8,128)(2,1)S(1)} custom-call(bf16[1,256,128]{2,1,0:T(8,128)(2,1)} %keys.1, bf16[1,256,128]{2,1,0:T(8,128)(2,1)} %values.1, s32[1,256]{1,0:T(1,128)} %bitcast.1), custom_call_target="tpu_custom_call" | custom-call | flops 5368709120 | bytes 132096 | tf_op jit(solution)/shard_map/pack/pallas_call | solution.py:230
  2.2 2.6 %collective-permute-start.1 = (bf16[272,256]{1,0:T(8,128)(2,1)S(1)}, bf16[272,256]{1,0:T(8,128)(2,1)S(1)}, u32[]{:S(2)}, u32[]{:S(2)}) collective-permute-start(bf16[272,256]{1,0:T(8,128)(2,1)S(1)} %pack.1.block.own), channel_id=1, source_target_pairs={{0,1},{1,2},{2,3},{3,4},{4,5},{5,6},{6,7},{7,8},{8,9},{9,10},{10,1... | collective-permute-start | bytes 417800 | tf_op jit(solution)/shard_map/ppermute | solution.py:67
  4.8 0.0 collective-permute-start.2
  4.8 0.0 collective-permute-done.grads
  4.8 0.0 copy-done
  4.8 0.0 copy-done.1
  4.8 0.0 copy-done.2
  4.8 1.6 %own_block.1 = (bf16[256,2048]{1,0:T(8,128)(2,1)S(1)}, f32[256,256]{1,0:T(8,128)S(1)}, f32[16,256]{1,0:T(8,128)S(1)}, bf16[272,256]{1,0:T(8,128)(2,1)S(1)}) custom-call(bf16[1,256,1024]{2,1,0:T(8,128)(2,1)S(1)} %copy-done.1, bf16[1,256,1024]{2,1,0:T(8,128)(2,1)S(1)} %copy-done, bf16[1,256,1024]{2,1,0:T(8,128)(2,1)S(1)} %collective-permute-done.grads, ...), custom_call_target="tpu_custom_call" | custom-call | flops 536870912 | bytes 1720320 | tf_op jit(solution)/shard_map/own_block/pallas_call | solution.py:230
  6.5 3.1 %collective-permute-start.3 = (bf16[272,256]{1,0:T(8,128)(2,1)S(1)}, bf16[272,256]{1,0:T(8,128)(2,1)S(1)}, u32[]{:S(2)}, u32[]{:S(2)}) collective-permute-start(bf16[272,256]{1,0:T(8,128)(2,1)S(1)} %get-tuple-element.19), channel_id=1, source_target_pairs={{0,2},{1,3},{2,4},{3,5},{4,6},{5,7},{6,8},{7,9},{8,10},{9,11},{10,... | collective-permute-start | bytes 417800 | tf_op jit(solution)/shard_map/ppermute | solution.py:67
  9.6 0.0 collective-permute-start.4
  9.6 0.0 collective-permute-done.1.refs_0_
  9.6 1.1 %collective-permute-done.2.refs_1_ = bf16[272,256]{1,0:T(8,128)(2,1)S(1)} collective-permute-done((bf16[272,256]{1,0:T(8,128)(2,1)S(1)}, bf16[272,256]{1,0:T(8,128)(2,1)S(1)}, u32[]{:S(2)}, u32[]{:S(2)}) %collective-permute-start.2) | collective-permute-done | bytes 139296 | tf_op jit(solution)/shard_map/ppermute | solution.py:67
  10.7 0.2 %near_block.1 = (bf16[256,2048]{1,0:T(8,128)(2,1)S(1)}, bf16[256,256]{1,0:T(8,128)(2,1)S(1)}, bf16[272,256]{1,0:T(8,128)(2,1)S(1)}) custom-call(bf16[1,256,1024]{2,1,0:T(8,128)(2,1)S(1)} %copy-done.1, bf16[1,256,1024]{2,1,0:T(8,128)(2,1)S(1)} %collective-permute-done.grads, f32[1,8,256]{2,1,0:T(8,128)S(1)} %copy-done.2, ...), custom_call_target="tpu_custom_call" | custom-call | flops 536870912 | bytes 1753088 | tf_op jit(solution)/shard_map/near_block/pallas_call | solution.py:230
  11.0 1.3 %collective-permute-start.5 = (bf16[256,256]{1,0:T(8,128)(2,1)S(1)}, bf16[256,256]{1,0:T(8,128)(2,1)S(1)}, u32[]{:S(2)}, u32[]{:S(2)}) collective-permute-start(bf16[256,256]{1,0:T(8,128)(2,1)S(1)} %get-tuple-element.18.before), channel_id=1, source_target_pairs={{1,0},{2,1},{3,2},{4,3},{5,4},{6,5},{7,6},{8,7},{9,8},{10,9},{11,1... | collective-permute-start | bytes 393224 | tf_op jit(solution)/shard_map/ppermute | solution.py:33
  12.3 0.6 %collective-permute-done.3.refs_0_ = bf16[272,256]{1,0:T(8,128)(2,1)S(1)} collective-permute-done((bf16[272,256]{1,0:T(8,128)(2,1)S(1)}, bf16[272,256]{1,0:T(8,128)(2,1)S(1)}, u32[]{:S(2)}, u32[]{:S(2)}) %collective-permute-start.3) | collective-permute-done | bytes 139296 | tf_op jit(solution)/shard_map/ppermute | solution.py:67
  12.8 1.8 %collective-permute-done.4.refs_1_ = bf16[272,256]{1,0:T(8,128)(2,1)S(1)} collective-permute-done((bf16[272,256]{1,0:T(8,128)(2,1)S(1)}, bf16[272,256]{1,0:T(8,128)(2,1)S(1)}, u32[]{:S(2)}, u32[]{:S(2)}) %collective-permute-start.4) | collective-permute-done | bytes 139296 | tf_op jit(solution)/shard_map/ppermute | solution.py:67
  14.7 0.2 far_block.1
  14.9 1.3 %collective-permute-start.6 = (bf16[256,256]{1,0:T(8,128)(2,1)S(1)}, bf16[256,256]{1,0:T(8,128)(2,1)S(1)}, u32[]{:S(2)}, u32[]{:S(2)}) collective-permute-start(bf16[256,256]{1,0:T(8,128)(2,1)S(1)} %get-tuple-element.24), channel_id=1, source_target_pairs={{2,0},{3,1},{4,2},{5,3},{6,4},{7,5},{8,6},{9,7},{10,8},{11,9},{12,... | collective-permute-start | bytes 393224 | tf_op jit(solution)/shard_map/ppermute | solution.py:33
  16.2 1.5 %query_grads.1 = bf16[1,256,1024]{2,1,0:T(8,128)(2,1)} custom-call(bf16[272,256]{1,0:T(8,128)(2,1)S(1)} %pack.1.block.own, bf16[272,256]{1,0:T(8,128)(2,1)S(1)} %get-tuple-element.17.near, bf16[272,256]{1,0:T(8,128)(2,1)S(1)} %get-tuple-element.20.far, bf16[256,2048]{1,0:T(8,128)(2,1)S(1)} %get-tuple-element.21.own_grads, ...), custom_call_target="tpu_custom_call" | custom-call | flops 402653184 | bytes 3563520 | tf_op jit(solution)/shard_map/query_grads/pallas_call | solution.py:230
  17.7 0.8 %collective-permute-done.5.near_sums = bf16[256,256]{1,0:T(8,128)(2,1)S(1)} collective-permute-done((bf16[256,256]{1,0:T(8,128)(2,1)S(1)}, bf16[256,256]{1,0:T(8,128)(2,1)S(1)}, u32[]{:S(2)}, u32[]{:S(2)}) %collective-permute-start.5) | collective-permute-done | bytes 131104 | tf_op jit(solution)/shard_map/ppermute | solution.py:33
  18.5 3.4 %collective-permute-done.6.far_sums = bf16[256,256]{1,0:T(8,128)(2,1)S(1)} collective-permute-done((bf16[256,256]{1,0:T(8,128)(2,1)S(1)}, bf16[256,256]{1,0:T(8,128)(2,1)S(1)}, u32[]{:S(2)}, u32[]{:S(2)}) %collective-permute-start.6) | collective-permute-done | bytes 131104 | tf_op jit(solution)/shard_map/ppermute | solution.py:33
  21.8 0.7 %add.1 = (bf16[1,256,128]{2,1,0:T(8,128)(2,1)}, bf16[1,256,128]{2,1,0:T(8,128)(2,1)}) custom-call(f32[256,256]{1,0:T(8,128)S(1)} %get-tuple-element.16.before.own_sums, bf16[256,256]{1,0:T(8,128)(2,1)S(1)} %collective-permute-done.5.near_sums, bf16[256,256]{1,0:T(8,128)(2,1)S(1)} %collective-permute-done.6.far_sums), custom_call_target="tpu_custom_call" | custom-call | bytes 524288 | tf_op jit(solution)/shard_map/add/pallas_call | solution.py:230
Async XLA Ops:
  0.6 4.2 %collective-permute-start = (bf16[1,256,1024]{2,1,0:T(8,128)(2,1)}, bf16[1,256,1024]{2,1,0:T(8,128)(2,1)S(1)}, u32[]{:S(2)}, u32[]{:S(2)}) collective-permute-start(bf16[1,256,1024]{2,1,0:T(8,128)(2,1)} %param.12), channel_id=1, source_target_pairs={{16,0},{0,16},{17,1},{1,17},{18,2},{2,18},{19,3},{3,19},{20,4},{4,... | collective-permute-start | bytes 1572872 | tf_op jit(solution)/shard_map/ppermute | solution.py:27
  1.2 3.6 %copy-start = (bf16[1,256,1024]{2,1,0:T(8,128)(2,1)S(1)}, bf16[1,256,1024]{2,1,0:T(8,128)(2,1)}, u32[]{:S(2)}) copy-start(bf16[1,256,1024]{2,1,0:T(8,128)(2,1)} %attn_out.1) | copy-start | bytes 1572868
  1.2 3.6 %copy-start.1 = (bf16[1,256,1024]{2,1,0:T(8,128)(2,1)S(1)}, bf16[1,256,1024]{2,1,0:T(8,128)(2,1)}, u32[]{:S(2)}) copy-start(bf16[1,256,1024]{2,1,0:T(8,128)(2,1)} %queries.5) | copy-start | bytes 1572868
  1.2 3.6 %copy-start.2 = (f32[1,8,256]{2,1,0:T(8,128)S(1)}, f32[1,8,256]{2,1,0:T(8,128)}, u32[]{:S(2)}) copy-start(f32[1,8,256]{2,1,0:T(8,128)} %log_sums.5) | copy-start | bytes 24580
  2.2 7.4 %collective-permute-start.1 = (bf16[272,256]{1,0:T(8,128)(2,1)S(1)}, bf16[272,256]{1,0:T(8,128)(2,1)S(1)}, u32[]{:S(2)}, u32[]{:S(2)}) collective-permute-start(bf16[272,256]{1,0:T(8,128)(2,1)S(1)} %pack.1.block.own), channel_id=1, source_target_pairs={{0,1},{1,2},{2,3},{3,4},{4,5},{5,6},{6,7},{7,8},{8,9},{9,10},{10,1... | collective-permute-start | bytes 417800 | tf_op jit(solution)/shard_map/ppermute | solution.py:67
  4.8 6.0 %collective-permute-start.2 = (bf16[272,256]{1,0:T(8,128)(2,1)S(1)}, bf16[272,256]{1,0:T(8,128)(2,1)S(1)}, u32[]{:S(2)}, u32[]{:S(2)}) collective-permute-start(bf16[272,256]{1,0:T(8,128)(2,1)S(1)} %pack.1.block.own), channel_id=1, source_target_pairs={{0,16},{1,5},{2,6},{3,0},{4,8},{5,1},{6,2},{7,3},{8,12},{9,13},{10... | collective-permute-start | bytes 417800 | tf_op jit(solution)/shard_map/ppermute | solution.py:67
  6.5 6.4 %collective-permute-start.3 = (bf16[272,256]{1,0:T(8,128)(2,1)S(1)}, bf16[272,256]{1,0:T(8,128)(2,1)S(1)}, u32[]{:S(2)}, u32[]{:S(2)}) collective-permute-start(bf16[272,256]{1,0:T(8,128)(2,1)S(1)} %get-tuple-element.19), channel_id=1, source_target_pairs={{0,2},{1,3},{2,4},{3,5},{4,6},{5,7},{6,8},{7,9},{8,10},{9,11},{10,... | collective-permute-start | bytes 417800 | tf_op jit(solution)/shard_map/ppermute | solution.py:67
  9.6 5.1 %collective-permute-start.4 = (bf16[272,256]{1,0:T(8,128)(2,1)S(1)}, bf16[272,256]{1,0:T(8,128)(2,1)S(1)}, u32[]{:S(2)}, u32[]{:S(2)}) collective-permute-start(bf16[272,256]{1,0:T(8,128)(2,1)S(1)} %get-tuple-element.19), channel_id=1, source_target_pairs={{0,16},{1,17},{2,0},{3,1},{4,5},{5,4},{6,2},{7,3},{8,9},{9,8},{10,... | collective-permute-start | bytes 417800 | tf_op jit(solution)/shard_map/ppermute | solution.py:67
  11.0 7.5 %collective-permute-start.5 = (bf16[256,256]{1,0:T(8,128)(2,1)S(1)}, bf16[256,256]{1,0:T(8,128)(2,1)S(1)}, u32[]{:S(2)}, u32[]{:S(2)}) collective-permute-start(bf16[256,256]{1,0:T(8,128)(2,1)S(1)} %get-tuple-element.18.before), channel_id=1, source_target_pairs={{1,0},{2,1},{3,2},{4,3},{5,4},{6,5},{7,6},{8,7},{9,8},{10,9},{11,1... | collective-permute-start | bytes 393224 | tf_op jit(solution)/shard_map/ppermute | solution.py:33
  14.9 7.0 %collective-permute-start.6 = (bf16[256,256]{1,0:T(8,128)(2,1)S(1)}, bf16[256,256]{1,0:T(8,128)(2,1)S(1)}, u32[]{:S(2)}, u32[]{:S(2)}) collective-permute-start(bf16[256,256]{1,0:T(8,128)(2,1)S(1)} %get-tuple-element.24), channel_id=1, source_target_pairs={{2,0},{3,1},{4,2},{5,3},{6,4},{7,5},{8,6},{9,7},{10,8},{11,9},{12,... | collective-permute-start | bytes 393224 | tf_op jit(solution)/shard_map/ppermute | solution.py:33

commit v6 on v5

v6 whole, which is shorter than its diff:
```python
import functools

import jax
import jax.numpy as jnp
from jax import lax
from jax.experimental import pallas as pl
from jax.experimental.pallas import tpu as pltpu
from jax.sharding import PartitionSpec as P

HOPS = 2
ORDERS = ((2, 1), (1, 2))
DOC_ROWS = 16
LAST_ROW = 8
COUNT_ROW = 9
FACT_ROWS = 8
NONE, FEW_KEYS, FEW_QUERIES, ALL = range(4)
BACK_STRIDE = 4
EARLY_HEADS = 6
LOG2_E = 1.4426950408889634
MASKED = -1e30

F32 = jnp.float32
BF16 = jnp.bfloat16


def from_behind(block, axis, distance):
    devices = range(lax.axis_size(axis))
    route = [((i - distance) % len(devices), i) for i in devices]
    return lax.ppermute(block, axis, route)


def full_routes(sections, shards, by, parity):
    route = {}
    for at in range(0, sections, 2):
        there, back = at + parity, at + 1 - parity
        for c in range(shards - by):
            route[there, c] = (there, c + by)
        free = set(range(shards))
        for last in range(shards - by, shards):
            first = last - shards + by
            way = [(there, last)] + [(back, c) for c in range(last, by - 1, -BACK_STRIDE)] + [(back, first), (there, first)]
            free -= {c for section, c in way if section == back}
            route.update(zip(way, way[1:]))
        for lane in range(BACK_STRIDE):
            rest = [c for c in sorted(free) if c % BACK_STRIDE == lane]
            pairs = [(c, c + 1) for c in rest if c + 1 in free] if by > 1 else []
            if by == 1:
                pairs = list(zip(rest[0::2], rest[1::2])) if len(rest) % 2 == 0 else []
                if not pairs:
                    route.update({(back, c): (back, rest[k - len(rest) + 1]) for k, c in enumerate(rest)})
            for c, d in pairs:
                route.update({(back, c): (back, d), (back, d): (back, c)})
    full = sections * shards
    whole = len(route) == full and len(set(route.values())) == full and all(a != b for a, b in route.items())
    return [(a * shards + c, b * shards + d) for (a, c), (b, d) in sorted(route.items())] if whole else None


def routes_behind(sections, shards, hop, parity):
    whole = sections % 2 == 0 and shards >= 4 * BACK_STRIDE
    route = full_routes(sections, shards, hop, parity) if whole else None
    if route is None:
        route = [(s * shards + c, s * shards + c + hop) for s in range(parity, sections, 2) for c in range(shards - hop)]
    return route


def returned(sums, order, ring):
    sections, shards = lax.axis_size("section"), lax.axis_size("ctx")
    hops = [order[s % 2] for s in range(sections)]
    pairs = [(s * shards + c, s * shards + (c - hops[s]) % shards) for s in range(sections) for c in range(0 if ring else hops[s], shards)]
    return lax.ppermute(sums, ("section", "ctx"), pairs)


def dot_nt(a, b):
    return lax.dot_general(a, b, (((1,), (1,)), ((), ())), preferred_element_type=F32)


def dot_nn(a, b):
    return lax.dot_general(a, b, (((1,), (0,)), ((), ())), preferred_element_type=F32)


def pack_kernel(keys, values, docs, packed, docs_here, sems):
    rows, width = keys.shape[1:]
    copies = [
        pltpu.make_async_copy(docs, docs_here, sems.at[0]),
        pltpu.make_async_copy(keys.at[0], packed.at[0:rows, 0:width], sems.at[1]),
        pltpu.make_async_copy(values.at[0], packed.at[0:rows, width : 2 * width], sems.at[2]),
    ]
    for copy in copies:
        copy.start()
    copies[0].wait()
    docs_row = docs_here[...]
    last = jnp.max(docs_row, axis=1, keepdims=True)
    last_count = jnp.sum((docs_row == last).astype(F32), axis=1, keepdims=True)
    row_at = lax.broadcasted_iota(jnp.int32, (DOC_ROWS, rows), 0)
    table = jnp.where(row_at == LAST_ROW, last.astype(F32) + 1, jnp.where(row_at == COUNT_ROW, last_count, docs_row.astype(F32) + 1))
    packed[rows : rows + DOC_ROWS, :] = table.astype(BF16)
    for copy in copies[1:]:
        copy.wait()


def column_of(row, width):
    rows = row.shape[1]
    column = jnp.transpose(jnp.broadcast_to(row, (width, rows)))
    return jnp.concatenate([column] * (rows // width), axis=1)


def block_grads(queries, grads, log_sums, delta_of, block, bias, score_grads, weights_low, sums, first_key, query_rows, chosen=None):
    rows = queries.shape[1]
    width = block.shape[1] // 2
    chosen = range(log_sums.shape[1]) if chosen is None else chosen
    scale = float(width) ** -0.5
    beside = rows // query_rows
    key_rows = slice(first_key, rows)
    side = lambda pieces: pieces[0] if len(pieces) == 1 else jnp.concatenate(pieces, axis=1)
    under = lambda pieces: pieces[0] if len(pieces) == 1 else jnp.concatenate(pieces, axis=0)
    part = lambda ref, head: ref[0, 0:query_rows, head * width : (head + 1) * width]
    columns = lambda head: slice(head * rows, head * rows + query_rows)
    masked = side([bias[key_rows, 0:query_rows]] * beside)
    for head in chosen[::beside]:
        group = range(head, head + beside)
        g = under([part(grads, h) for h in group])
        delta = side([delta_of(h, part(grads, h))[:, 0:query_rows] for h in group])
        lse = side([log_sums[0, h : h + 1, 0:query_rows] for h in group]) * LOG2_E
        scores = dot_nt(block[key_rows, 0:width], under([part(queries, h) for h in group]))
        weights = jnp.exp2(scores * (scale * LOG2_E) - lse + masked)
        weight_grads = dot_nt(block[key_rows, width : 2 * width], g)
        low = (weights * (weight_grads - delta)).astype(BF16)
        weights = weights.astype(BF16)
        for at, h in enumerate(group):
            here = slice(at * query_rows, (at + 1) * query_rows)
            score_grads[key_rows, columns(h)] = low[:, here]
            weights_low[key_rows, columns(h)] = weights[:, here]
    straight = slice(chosen[0] * rows, (chosen[-1] + 1) * rows)
    everything = lambda ref: ref[key_rows, straight] if beside == 1 else side([ref[key_rows, columns(h)] for h in chosen])
    stacked = lambda ref: under([part(ref, h) for h in chosen])
    sums[key_rows, 0:width] = (dot_nn(everything(score_grads), stacked(queries)) * scale).astype(sums.dtype)
    sums[key_rows, width : 2 * width] = dot_nn(everything(weights_low), stacked(grads)).astype(sums.dtype)


def own_bias(block, bias):
    rows = bias.shape[0]
    docs = block[rows : rows + DOC_ROWS, :].astype(F32)[0:1]
    key_at = lax.broadcasted_iota(jnp.int32, (rows, rows), 0)
    query_at = lax.broadcasted_iota(jnp.int32, (rows, rows), 1)
    bias[...] = jnp.where((column_of(docs, block.shape[1] // 2) == docs) & (key_at <= query_at), 0.0, MASKED)


def own_kernel(chosen, queries, attn_out, grads, log_sums, block, score_grads, sums, deltas, block_again, bias, weights_low):
    rows = queries.shape[1]
    heads = log_sums.shape[1]
    width = block.shape[1] // 2
    block_again[...] = block[...]
    docs = block[rows : rows + DOC_ROWS, :].astype(F32)[0:1]
    first_count = jnp.sum((docs == docs[:, 0:1]).astype(F32), axis=1, keepdims=True)
    deltas[heads:, :] = jnp.broadcast_to(first_count, (FACT_ROWS, rows))
    own_bias(block, bias)
    one = jnp.ones((8, width), BF16)
    for head in range(heads):
        part = slice(head * width, (head + 1) * width)
        product = grads[0, :, part].astype(F32) * attn_out[0, :, part].astype(F32)
        high = product.astype(BF16)
        low = (product - high.astype(F32)).astype(BF16)
        deltas[head : head + 1, :] = (dot_nt(one, high) + dot_nt(one, low))[0:1]
    delta_of = lambda head, g: deltas[head : head + 1, :]
    block_grads(queries, grads, log_sums, delta_of, block, bias, score_grads, weights_low, sums, 0, rows, chosen)


def rest_kernel(chosen, queries, grads, log_sums, deltas, block, before, first_grads, score_grads, sums, bias, weights_low):
    own_bias(block, bias)
    delta_of = lambda head, g: deltas[head : head + 1, :]
    block_grads(queries, grads, log_sums, delta_of, block, bias, score_grads, weights_low, sums, 0, queries.shape[1], chosen)


def hop_kernel(hop, parity, queries, grads, log_sums, deltas, own, block, before, *refs):
    score_grads, sums, bias, weights_low = refs[-4:]

    def reachable():
        rows = queries.shape[1]
        half = rows // 2
        docs = own[rows : rows + DOC_ROWS, :].astype(F32)[0:1]
        table = block[rows : rows + DOC_ROWS, :].astype(F32)
        same = (table[LAST_ROW : LAST_ROW + 1] == docs[:, 0:1]) & (lax.axis_index("ctx") >= hop)
        key_count = jnp.where(same, table[COUNT_ROW : COUNT_ROW + 1], 0.0)
        query_count = deltas[log_sums.shape[1] : log_sums.shape[1] + 1, :]
        key_at = lax.broadcasted_iota(jnp.int32, (rows, rows), 0).astype(F32)
        bias[...] = jnp.where((key_at >= rows - key_count) & (docs == docs[:, 0:1]), 0.0, MASKED)
        some = jnp.where(query_count <= half, FEW_QUERIES, ALL)
        mode = jnp.where(key_count == 0, NONE, jnp.where(key_count <= half, FEW_KEYS, some))[0, 0]
        delta_of = lambda head, g: deltas[head : head + 1, :]
        work = functools.partial(block_grads, queries, grads, log_sums, delta_of, block, bias, score_grads, weights_low, sums)

        @pl.when(mode == NONE)
        def _():
            score_grads[...] = jnp.zeros_like(score_grads)
            sums[...] = jnp.zeros_like(sums)

        @pl.when(mode == FEW_KEYS)
        def _():
            score_grads[0:half, :] = jnp.zeros((half, score_grads.shape[1]), BF16)
            sums[0:half, :] = jnp.zeros((half, sums.shape[1]), BF16)
            work(half, rows)

        @pl.when(mode == FEW_QUERIES)
        def _():
            for head in range(score_grads.shape[1] // rows):
                score_grads[:, head * rows + half : (head + 1) * rows] = jnp.zeros((rows, rows - half), BF16)
            work(0, half)

        if hop < HOPS:

            @pl.when(mode == ALL)
            def _():
                work(0, rows)

    pl.when(lax.axis_index("section") % 2 == parity)(reachable)


def pick(candidates, block):
    for parity, candidate in enumerate(candidates):

        @pl.when(lax.axis_index("section") % 2 == parity)
        def _():
            block[...] = candidate[...]


def query_kernel(own, own_grads, first_grads, second_grads, first_even, first_odd, second_even, second_odd, grad_queries, first, second):
    pick((first_even, first_odd), first)
    pick((second_even, second_odd), second)
    rows = own_grads.shape[0]
    heads = own_grads.shape[1] // rows
    width = own.shape[1] // 2
    scale = float(width) ** -0.5
    turned = [jnp.transpose(block[0:rows, 0:width].astype(F32)).astype(BF16) for block in (own, first, second)]
    for head in range(heads):
        columns = slice(head * rows, (head + 1) * rows)
        total = dot_nn(turned[0], own_grads[:, columns]) + dot_nn(turned[1], first_grads[:, columns]) + dot_nn(turned[2], second_grads[:, columns])
        grad_queries[0, :, head * width : (head + 1) * width] = jnp.transpose(total * scale).astype(BF16)


def add_kernel(shards, own_sums, rest_sums, first_sums, second_sums, grad_keys, grad_values):
    width = grad_keys.shape[2]
    total = own_sums[...] + rest_sums[...]
    for order, part in zip(ORDERS, (first_sums, second_sums)):
        hop = jnp.where(lax.axis_index("section") % 2 == 0, *order)
        total = total + jnp.where(lax.axis_index("ctx") + hop < shards, part[...].astype(F32), 0.0)
    grad_keys[0] = total[:, 0:width].astype(BF16)
    grad_values[0] = total[:, width : 2 * width].astype(BF16)


def call(kernel, name, outs, args, flops=0, scratch=(), from_hbm=0, kept=(), limit=8):
    args = [pltpu.with_memory_space_constraint(a, pltpu.HBM) for a in args[:from_hbm]] + list(args[from_hbm:])
    moved = sum(a.size * a.dtype.itemsize for a in args)
    vmem = lambda count: [pl.BlockSpec(memory_space=pltpu.VMEM)] * count
    return pl.pallas_call(
        kernel,
        out_shape=outs,
        in_specs=[pl.BlockSpec(memory_space=pltpu.HBM)] * from_hbm + vmem(len(args) - from_hbm + len(kept)),
        out_specs=tuple(vmem(len(outs))),
        scratch_shapes=list(scratch),
        input_output_aliases={len(args) + i: i for i in range(len(kept))},
        compiler_params=pltpu.CompilerParams(vmem_limit_bytes=limit * 1024 * 1024),
        cost_estimate=pl.CostEstimate(flops=flops, bytes_accessed=moved, transcendentals=0),
        name=name,
    )(*args, *kept)


def per_device(queries, keys, values, attn_out, log_sums, grad_held, doc_ids):
    rows, width = keys.shape[1:]
    heads = log_sums.shape[1]
    shape = jax.ShapeDtypeStruct
    flops = 2 * heads * rows * rows * width
    score_grads = shape((rows, heads * rows), BF16)
    scratch = [pltpu.VMEM((rows, rows), F32), pltpu.VMEM((rows, heads * rows), BF16)]
    sums = lambda dtype: shape((rows, 2 * width), dtype)

    grads = from_behind(grad_held, "section", -1)
    (own,) = call(
        pack_kernel,
        "pack",
        (shape((rows + DOC_ROWS, 2 * width), BF16),),
        (keys, values, doc_ids.reshape(1, rows)),
        40 * flops,
        [pltpu.VMEM((1, rows), jnp.int32), pltpu.SemaphoreType.DMA((3,))],
        3,
    )
    sections, shards = lax.axis_size("section"), lax.axis_size("ctx")
    behind = lambda block, order: [
        lax.ppermute(block, ("section", "ctx"), routes_behind(sections, shards, hop, parity)) for parity, hop in enumerate(order)
    ]
    first_order, second_order = ORDERS
    first = behind(own, first_order)
    early = range(EARLY_HEADS * heads // 8)
    late = range(len(early), heads)
    own_grads, own_sums, deltas, own_again = call(
        functools.partial(own_kernel, early),
        "own_block",
        (score_grads, sums(F32), shape((heads + FACT_ROWS, rows), F32), shape(own.shape, BF16)),
        (queries, attn_out, grads, log_sums, own),
        4 * flops,
        scratch,
    )
    second = behind(own_again, second_order)

    def block_of(name, order, before, candidates):
        kept = ()
        for parity, (hop, block) in enumerate(zip(order, candidates)):
            args = (queries, grads, log_sums, deltas, own, block, before)
            kept = call(functools.partial(hop_kernel, hop, parity), name, (score_grads, sums(BF16)), args, 4 * flops, scratch, 0, kept)
        return kept

    first_grads, first_sums = block_of("first_block", first_order, own_sums, first)
    first_back = returned(first_sums, first_order, True)
    second_grads, second_sums = block_of("second_block", second_order, first_sums, second)
    second_back = returned(second_sums, second_order, True)
    own_grads, rest_sums = call(
        functools.partial(rest_kernel, late),
        "own_rest",
        (score_grads, sums(F32)),
        (queries, grads, log_sums, deltas, own, second_sums),
        2 * flops,
        scratch,
        0,
        (own_grads,),
    )
    (grad_queries,) = call(
        query_kernel,
        "query_grads",
        (shape(queries.shape, BF16),),
        (own, own_grads, first_grads, second_grads, *first, *second),
        3 * flops,
        [pltpu.VMEM(own.shape, BF16)] * 2,
    )
    grad_keys, grad_values = call(
        functools.partial(add_kernel, shards), "add", (shape(keys.shape, BF16), shape(values.shape, BF16)), (own_sums, rest_sums, first_back, second_back)
    )
    return grad_queries, grad_keys, grad_values


def solution(mesh):
    placed = (
        P("section", "ctx", None),
        P("section", "ctx", None),
        P("section", "ctx", None),
        P("section", "ctx", None),
        P("section", None, "ctx"),
        P("section", "ctx", None),
        P("ctx"),
    )
    return jax.shard_map(
        per_device,
        mesh=mesh,
        in_specs=placed,
        out_specs=(P("section", "ctx", None), P("section", "ctx", None), P("section", "ctx", None)),
        check_vma=False,
    )
```

time: 22.8 us -> 22.2 us (0.974)
  waiting for transfers between devices: 7.67 us -> 1.7 us
  starting transfers between devices: 8.82 us -> 14 us
  Pallas kernels: 5.3 us -> 5.63 us
    ppermute x6, waiting for transfers between devices: 7.66 us -> 1.69 us  [the longest x4 1.24 us: per_device(): lax.ppermute(block, ('section', 'ctx'), routes_behind(sections, shards, h...]
    ppermute x6, starting transfers between devices: 8.31 us -> 13.5 us  [the longest x2 7.79 us: returned(): return lax.ppermute(sums, ('section', 'ctx'), pairs)]
    pallas_call x6 -> x9, Pallas kernels: 5.3 us -> 5.63 us  [call(): pl.pallas_call(kernel, out_shape=outs, in_specs=[pl.BlockSpec(memory_spac...]
  transfers between devices with their start and end apart: 7 -> 7, of which waited for: 5 -> 2; matrix products, arithmetic and copies ran while one was open for 0% -> 0% of each run, Pallas kernels for 21% -> 22%
where the time goes in v6:
time: 22.2 us; the launch traced here: 22.1 us
  starting transfers between devices  14 us (63%)
  Pallas kernels  5.63 us (25%)
  waiting for transfers between devices  1.7 us (8%)
  between operations  0.71 us (3%)
    ppermute x2, starting transfers between devices, returned(): return lax.ppermute(sums, ('section', 'ctx'), pairs)  7.79 us
    ppermute x4, starting transfers between devices, per_device(): lax.ppermute(block, ('section', 'ctx'), routes_behind(sections, shards, h...  5.72 us
    pallas_call x9, Pallas kernels, call(): pl.pallas_call(kernel, out_shape=outs, in_specs=[pl.BlockSpec(memory_spac...  5.63 us
    ppermute x4, waiting for transfers between devices, per_device(): lax.ppermute(block, ('section', 'ctx'), routes_behind(sections, shards, h...  1.24 us
    ppermute x1, starting transfers between devices, from_behind(): return lax.ppermute(block, axis, route)  0.52 us
    ppermute x2, waiting for transfers between devices, returned(): return lax.ppermute(sums, ('section', 'ctx'), pairs)  0.46 us
  transfers between devices with their start and end apart: 7, of which 2 were waited for; matrix products, arithmetic and copies ran while one was open for 0% of the time, Pallas kernels for 22%

profile of v6, /device:TPU:0, one launch (start us, length us, event | category | flops | bytes accessed | tf_op | source)
XLA Modules:
  0.0 22.1 jit_solution(8489780692850924373)
XLA Ops:
  0.6 0.5 %collective-permute-start = (bf16[1,256,1024]{2,1,0:T(8,128)(2,1)}, bf16[1,256,1024]{2,1,0:T(8,128)(2,1)S(1)}, u32[]{:S(2)}, u32[]{:S(2)}) collective-permute-start(bf16[1,256,1024]{2,1,0:T(8,128)(2,1)} %param.12), channel_id=1, source_target_pairs={{16,0},{0,16},{17,1},{1,17},{18,2},{2,18},{19,3},{3,19},{20,4},{4,... | collective-permute-start | bytes 1572872 | tf_op jit(solution)/shard_map/ppermute | solution.py:29
  1.2 0.0 copy-start
  1.2 0.0 copy-start.1
  1.2 0.0 copy-start.2
  1.2 1.0 %pack.1.block.own = bf16[272,256]{1,0:T(8,128)(2,1)S(1)} custom-call(bf16[1,256,128]{2,1,0:T(8,128)(2,1)} %keys.1, bf16[1,256,128]{2,1,0:T(8,128)(2,1)} %values.1, s32[1,256]{1,0:T(1,128)} %bitcast.1), custom_call_target="tpu_custom_call" | custom-call | flops 5368709120 | bytes 132096 | tf_op jit(solution)/shard_map/pack/pallas_call | solution.py:254
  2.2 2.6 %collective-permute-start.3 = (bf16[272,256]{1,0:T(8,128)(2,1)S(1)}, bf16[272,256]{1,0:T(8,128)(2,1)S(1)}, u32[]{:S(2)}, u32[]{:S(2)}) collective-permute-start(bf16[272,256]{1,0:T(8,128)(2,1)S(1)} %pack.1.block.own), channel_id=1, source_target_pairs={{0,2},{1,3},{2,4},{3,5},{4,6},{5,7},{6,8},{7,9},{8,10},{9,11},{10,... | collective-permute-start | bytes 417800 | tf_op jit(solution)/shard_map/ppermute | solution.py:288
  4.8 0.0 collective-permute-start.2
  4.8 0.0 collective-permute-done.grads
  4.8 0.0 copy-done
  4.8 0.0 copy-done.1
  4.8 0.0 copy-done.2
  4.8 1.4 %own_block.1 = (bf16[256,2048]{1,0:T(8,128)(2,1)S(1)}, f32[256,256]{1,0:T(8,128)S(1)}, f32[16,256]{1,0:T(8,128)S(1)}, bf16[272,256]{1,0:T(8,128)(2,1)S(1)}) custom-call(bf16[1,256,1024]{2,1,0:T(8,128)(2,1)S(1)} %copy-done, bf16[1,256,1024]{2,1,0:T(8,128)(2,1)S(1)} %copy-done.2, bf16[1,256,1024]{2,1,0:T(8,128)(2,1)S(1)} %collective-permute-done.grads, ...), custom_call_target="tpu_custom_call" | custom-call | flops 536870912 | bytes 1720320 | tf_op jit(solution)/shard_map/own_block/pallas_call | solution.py:254
  6.2 3.1 %collective-permute-start.4 = (bf16[272,256]{1,0:T(8,128)(2,1)S(1)}, bf16[272,256]{1,0:T(8,128)(2,1)S(1)}, u32[]{:S(2)}, u32[]{:S(2)}) collective-permute-start(bf16[272,256]{1,0:T(8,128)(2,1)S(1)} %get-tuple-element.20), channel_id=1, source_target_pairs={{0,1},{1,2},{2,3},{3,4},{4,5},{5,6},{6,7},{7,8},{8,9},{9,10},{10,1... | collective-permute-start | bytes 417800 | tf_op jit(solution)/shard_map/ppermute | solution.py:288
  9.3 0.0 collective-permute-start.1
  9.3 0.0 collective-permute-done.3.block.first_even
  9.3 0.2 first_block.2
  9.5 1.2 %collective-permute-done.2.block.first_odd = bf16[272,256]{1,0:T(8,128)(2,1)S(1)} collective-permute-done((bf16[272,256]{1,0:T(8,128)(2,1)S(1)}, bf16[272,256]{1,0:T(8,128)(2,1)S(1)}, u32[]{:S(2)}, u32[]{:S(2)}) %collective-permute-start.2) | collective-permute-done | bytes 139296 | tf_op jit(solution)/shard_map/ppermute | solution.py:288
  10.8 4.3 %collective-permute-start.5 = (bf16[256,256]{1,0:T(8,128)(2,1)S(1)}, bf16[256,256]{1,0:T(8,128)(2,1)S(1)}, u32[]{:S(2)}, u32[]{:S(2)}) collective-permute-start(bf16[256,256]{1,0:T(8,128)(2,1)S(1)} %get-tuple-element.24.before), channel_id=1, source_target_pairs={{0,14},{1,15},{2,0},{3,1},{4,2},{5,3},{6,4},{7,5},{8,6},{9,7},{10,... | collective-permute-start | bytes 393224 | tf_op jit(solution)/shard_map/ppermute | solution.py:70
  15.1 0.0 collective-permute-done.4.block.second_even
  15.1 0.2 second_block.2
  15.3 0.0 collective-permute-done.1.block.second_odd
  15.4 3.5 %collective-permute-start.6 = (bf16[256,256]{1,0:T(8,128)(2,1)S(1)}, bf16[256,256]{1,0:T(8,128)(2,1)S(1)}, u32[]{:S(2)}, u32[]{:S(2)}) collective-permute-start(bf16[256,256]{1,0:T(8,128)(2,1)S(1)} %get-tuple-element.27.before), channel_id=1, source_target_pairs={{0,15},{1,0},{2,1},{3,2},{4,3},{5,4},{6,5},{7,6},{8,7},{9,8},{10,9... | collective-permute-start | bytes 393224 | tf_op jit(solution)/shard_map/ppermute | solution.py:70
  18.8 0.5 %own_rest.1 = (bf16[256,2048]{1,0:T(8,128)(2,1)S(1)}, f32[256,256]{1,0:T(8,128)S(1)}) custom-call(bf16[1,256,1024]{2,1,0:T(8,128)(2,1)S(1)} %copy-done, bf16[1,256,1024]{2,1,0:T(8,128)(2,1)S(1)} %collective-permute-done.grads, f32[1,8,256]{2,1,0:T(8,128)S(1)} %copy-done.1, f32[16,256]{1,0:T(8,128)S(1)} %get-tuple-element.19.deltas, ...), custom_call_target="tpu_custom_call", output_to_operand_aliasing={{0}: (6, {})} | custom-call | flops 268435456 | bytes 1343488 | tf_op jit(solution)/shard_map/own_rest/pallas_call | solution.py:254
  19.3 1.6 %query_grads.1 = bf16[1,256,1024]{2,1,0:T(8,128)(2,1)} custom-call(bf16[272,256]{1,0:T(8,128)(2,1)S(1)} %pack.1.block.own, bf16[256,2048]{1,0:T(8,128)(2,1)S(1)} %get-tuple-element.29.own_grads, bf16[256,2048]{1,0:T(8,128)(2,1)S(1)} %get-tuple-element.30.first_grads, bf16[256,2048]{1,0:T(8,128)(2,1)S(1)} %get-tuple-element.31.second_grads, ...), custom_call_target="tpu_custom_call" | custom-call | flops 402653184 | bytes 3842048 | tf_op jit(solution)/shard_map/query_grads/pallas_call | solution.py:254
  20.9 0.0 collective-permute-done.5.first_sums
  20.9 0.5 %collective-permute-done.6.second_sums = bf16[256,256]{1,0:T(8,128)(2,1)S(1)} collective-permute-done((bf16[256,256]{1,0:T(8,128)(2,1)S(1)}, bf16[256,256]{1,0:T(8,128)(2,1)S(1)}, u32[]{:S(2)}, u32[]{:S(2)}) %collective-permute-start.6) | collective-permute-done | bytes 131104 | tf_op jit(solution)/shard_map/ppermute | solution.py:70
  21.3 0.7 %add.1 = (bf16[1,256,128]{2,1,0:T(8,128)(2,1)}, bf16[1,256,128]{2,1,0:T(8,128)(2,1)}) custom-call(f32[256,256]{1,0:T(8,128)S(1)} %get-tuple-element.21.before.own_sums, f32[256,256]{1,0:T(8,128)S(1)} %get-tuple-element.32.rest_sums, bf16[256,256]{1,0:T(8,128)(2,1)S(1)} %collective-permute-done.5.first_sums, ...), custom_call_target="tpu_custom_call" | custom-call | bytes 786432 | tf_op jit(solution)/shard_map/add/pallas_call | solution.py:254
  (2 shorter events, 0.0 us)
Async XLA Ops:
  0.6 4.2 %collective-permute-start = (bf16[1,256,1024]{2,1,0:T(8,128)(2,1)}, bf16[1,256,1024]{2,1,0:T(8,128)(2,1)S(1)}, u32[]{:S(2)}, u32[]{:S(2)}) collective-permute-start(bf16[1,256,1024]{2,1,0:T(8,128)(2,1)} %param.12), channel_id=1, source_target_pairs={{16,0},{0,16},{17,1},{1,17},{18,2},{2,18},{19,3},{3,19},{20,4},{4,... | collective-permute-start | bytes 1572872 | tf_op jit(solution)/shard_map/ppermute | solution.py:29
  1.2 3.7 %copy-start = (bf16[1,256,1024]{2,1,0:T(8,128)(2,1)S(1)}, bf16[1,256,1024]{2,1,0:T(8,128)(2,1)}, u32[]{:S(2)}) copy-start(bf16[1,256,1024]{2,1,0:T(8,128)(2,1)} %queries.11) | copy-start | bytes 1572868
  1.2 3.7 %copy-start.1 = (f32[1,8,256]{2,1,0:T(8,128)S(1)}, f32[1,8,256]{2,1,0:T(8,128)}, u32[]{:S(2)}) copy-start(f32[1,8,256]{2,1,0:T(8,128)} %log_sums.11) | copy-start | bytes 24580
  1.2 3.7 %copy-start.2 = (bf16[1,256,1024]{2,1,0:T(8,128)(2,1)S(1)}, bf16[1,256,1024]{2,1,0:T(8,128)(2,1)}, u32[]{:S(2)}) copy-start(bf16[1,256,1024]{2,1,0:T(8,128)(2,1)} %attn_out.1) | copy-start | bytes 1572868
  2.2 7.1 %collective-permute-start.3 = (bf16[272,256]{1,0:T(8,128)(2,1)S(1)}, bf16[272,256]{1,0:T(8,128)(2,1)S(1)}, u32[]{:S(2)}, u32[]{:S(2)}) collective-permute-start(bf16[272,256]{1,0:T(8,128)(2,1)S(1)} %pack.1.block.own), channel_id=1, source_target_pairs={{0,2},{1,3},{2,4},{3,5},{4,6},{5,7},{6,8},{7,9},{8,10},{9,11},{10,... | collective-permute-start | bytes 417800 | tf_op jit(solution)/shard_map/ppermute | solution.py:288
  4.8 6.0 %collective-permute-start.2 = (bf16[272,256]{1,0:T(8,128)(2,1)S(1)}, bf16[272,256]{1,0:T(8,128)(2,1)S(1)}, u32[]{:S(2)}, u32[]{:S(2)}) collective-permute-start(bf16[272,256]{1,0:T(8,128)(2,1)S(1)} %pack.1.block.own), channel_id=1, source_target_pairs={{0,16},{1,5},{2,6},{3,0},{4,8},{5,1},{6,2},{7,3},{8,12},{9,13},{10... | collective-permute-start | bytes 417800 | tf_op jit(solution)/shard_map/ppermute | solution.py:288
  6.2 8.9 %collective-permute-start.4 = (bf16[272,256]{1,0:T(8,128)(2,1)S(1)}, bf16[272,256]{1,0:T(8,128)(2,1)S(1)}, u32[]{:S(2)}, u32[]{:S(2)}) collective-permute-start(bf16[272,256]{1,0:T(8,128)(2,1)S(1)} %get-tuple-element.20), channel_id=1, source_target_pairs={{0,1},{1,2},{2,3},{3,4},{4,5},{5,6},{6,7},{7,8},{8,9},{9,10},{10,1... | collective-permute-start | bytes 417800 | tf_op jit(solution)/shard_map/ppermute | solution.py:288
  9.3 6.0 %collective-permute-start.1 = (bf16[272,256]{1,0:T(8,128)(2,1)S(1)}, bf16[272,256]{1,0:T(8,128)(2,1)S(1)}, u32[]{:S(2)}, u32[]{:S(2)}) collective-permute-start(bf16[272,256]{1,0:T(8,128)(2,1)S(1)} %get-tuple-element.20), channel_id=1, source_target_pairs={{0,16},{1,17},{2,0},{3,1},{4,5},{5,4},{6,2},{7,3},{8,9},{9,8},{10,... | collective-permute-start | bytes 417800 | tf_op jit(solution)/shard_map/ppermute | solution.py:288
  10.8 10.1 %collective-permute-start.5 = (bf16[256,256]{1,0:T(8,128)(2,1)S(1)}, bf16[256,256]{1,0:T(8,128)(2,1)S(1)}, u32[]{:S(2)}, u32[]{:S(2)}) collective-permute-start(bf16[256,256]{1,0:T(8,128)(2,1)S(1)} %get-tuple-element.24.before), channel_id=1, source_target_pairs={{0,14},{1,15},{2,0},{3,1},{4,2},{5,3},{6,4},{7,5},{8,6},{9,7},{10,... | collective-permute-start | bytes 393224 | tf_op jit(solution)/shard_map/ppermute | solution.py:70
  15.4 6.0 %collective-permute-start.6 = (bf16[256,256]{1,0:T(8,128)(2,1)S(1)}, bf16[256,256]{1,0:T(8,128)(2,1)S(1)}, u32[]{:S(2)}, u32[]{:S(2)}) collective-permute-start(bf16[256,256]{1,0:T(8,128)(2,1)S(1)} %get-tuple-element.27.before), channel_id=1, source_target_pairs={{0,15},{1,0},{2,1},{3,2},{4,3},{5,4},{6,5},{7,6},{8,7},{9,8},{10,9... | collective-permute-start | bytes 393224 | tf_op jit(solution)/shard_map/ppermute | solution.py:70
